TPU v7x, 32 devices: a whole 2x2x4 slice. The times are simulated.
32 devices in a mesh: pipe: 2 (over x), dp: 4 (over z), tensor: 4 (over y, core).
Axes of the slice: x: 2, y: 2, z: 4, core: 2. Of those that a mesh axis runs over, the one named last changes fastest.
Arguments:
- image_side: bfloat16 [2, 32, 197, 768], P('pipe', 'dp'), may hold values from -6 to 6
- text_side: bfloat16 [2, 8, 512, 768], P('pipe', 'dp'), may hold values from -6 to 6
- caption_lengths: int32 [8, 8], P('dp'), may hold values from 1 to 128, 512 in all within a row
- norm_gains: float32 [2, 2, 768], P('pipe'), may hold values from 0.25 to 1.75
- norm_shifts: float32 [2, 2, 768], P('pipe'), may hold values from -1.8 to 1.8
- w_qkv: bfloat16 [2, 768, 3, 768], P('pipe', None, None, 'tensor'), may hold values from -0.21875 to 0.21875
- bias_qv: float32 [2, 2, 768], P('pipe', None, 'tensor'), may hold values from -3 to 3
- w_proj: bfloat16 [2, 768, 768], P('pipe', 'tensor'), may hold values from -0.625 to 0.625
- out_bias: float32 [2, 2, 768], P('pipe'), may hold values from -1.8 to 1.8
- w_up: bfloat16 [2, 768, 3072], P('pipe', None, 'tensor'), may hold values from -0.21875 to 0.21875
- bias_up: float32 [2, 3072], P('pipe', 'tensor'), may hold values from -3 to 3
- w_down: bfloat16 [2, 3072, 768], P('pipe', 'tensor'), may hold values from -0.109375 to 0.109375
Outputs:
- image_result: bfloat16 [2, 32, 197, 768], P('pipe', 'dp')
- text_result: bfloat16 [2, 8, 512, 768], P('pipe', 'dp')
- gains_grad: float32 [2, 2, 768], P('pipe')
- shifts_grad: float32 [2, 2, 768], P('pipe')
- qkv_grad: float32 [2, 768, 3, 768], P('pipe', 'dp', None, 'tensor')
- bias_qv_grad: float32 [2, 2, 768], P('pipe', None, 'tensor')
- proj_grad: float32 [2, 768, 768], P('pipe', 'tensor', 'dp')
- out_bias_grad: float32 [2, 2, 768], P('pipe')
- up_grad: float32 [2, 768, 3072], P('pipe', 'dp', 'tensor')
- bias_up_grad: float32 [2, 3072], P('pipe', 'tensor')
- down_grad: float32 [2, 3072, 768], P('pipe', 'tensor', 'dp')
Inputs may be any that keep to these rules, and one draw needn't show every extreme that they name: `caption_lengths`: each row holds the lengths of the 8 captions packed into one text block; they sum to 512 and the largest is exactly 128.
All inputs are finite; a program needn't handle non-finite values.
Results may differ from a plain program's by a relative error of at most 0.014.
Values may be sent and summed in bfloat16 or wider, within the bound.
A program may use at most 192 MiB of HBM per device.

v0:
```python
from functools import partial

import jax
import jax.numpy as jnp
from jax import lax
from jax.sharding import PartitionSpec as P

HEAD_DIM = 64
MICRO = 2


epsilon = 1e-06
masked_score = -1000000000.0


def shifted(block, axis, distance):
    devices = range(lax.axis_size(axis))
    route = [(i - distance, i) for i in devices if i - distance in devices]
    return lax.ppermute(block, axis, route)


def norm_parts(rows_in, gain_row, shift_row):
    centre = rows_in - jnp.mean(rows_in, axis=-1, keepdims=True)
    inverse = lax.rsqrt(jnp.mean(centre * centre, axis=-1, keepdims=True) + epsilon)
    unit_rows = centre * inverse
    return (unit_rows * gain_row + shift_row, unit_rows, inverse)


def norm_back(grad_out, unit_rows, inverse, gain_row):
    scaled = grad_out * gain_row
    first_mean = jnp.mean(scaled, axis=-1, keepdims=True)
    second_mean = jnp.mean(scaled * unit_rows, axis=-1, keepdims=True)
    grad_in = inverse * (scaled - first_mean - unit_rows * second_mean)
    return (grad_in, jnp.sum(grad_out * unit_rows, axis=0), jnp.sum(grad_out, axis=0))


def caption_mask(lengths, length):
    bounds = jnp.cumsum(lengths, axis=-1)
    places = jnp.arange(length, dtype=jnp.int32)
    segment = jnp.sum((places[None, :, None] >= bounds[:, None, :]).astype(jnp.int32), axis=-1)
    return segment[:, :, None] == segment[:, None, :]


def attend(queries, key_rows, value_rows, allowed, number, length):
    heads_local = queries.shape[-1] // HEAD_DIM
    shape_four = (number, length, heads_local, HEAD_DIM)
    scores = jnp.einsum(
        "nqhe,nkhe->nhqk",
        queries.reshape(shape_four),
        key_rows.reshape(shape_four),
        preferred_element_type=jnp.float32,
    )
    scores = jnp.where(allowed[:, None], scores, masked_score)
    highest = jnp.max(scores, axis=-1, keepdims=True)
    raised = jnp.exp(scores - highest)
    row_total = jnp.sum(raised, axis=-1, keepdims=True)
    attn_weights = (raised / row_total).astype(jnp.bfloat16)
    log_total = highest + jnp.log(row_total)
    mixture = jnp.einsum(
        "nhqk,nkhe->nqhe",
        attn_weights,
        value_rows.reshape(shape_four),
        preferred_element_type=jnp.float32,
    )
    return (mixture.reshape(number * length, heads_local * HEAD_DIM), log_total)


def attend_back(queries, key_rows, value_rows, log_total, grad_mixture, allowed, number, length):
    heads_local = queries.shape[-1] // HEAD_DIM
    shape_four = (number, length, heads_local, HEAD_DIM)
    query_four = queries.reshape(shape_four)
    key_four = key_rows.reshape(shape_four)
    value_four = value_rows.reshape(shape_four)
    grad_four = grad_mixture.reshape(shape_four)
    scores = jnp.einsum("nqhe,nkhe->nhqk", query_four, key_four, preferred_element_type=jnp.float32)
    attn_weights = jnp.where(
        allowed[:, None],
        jnp.exp(jnp.where(allowed[:, None], scores, masked_score) - log_total),
        0.0,
    )
    grad_weights = jnp.einsum(
        "nqhe,nkhe->nhqk", grad_four, value_four, preferred_element_type=jnp.float32
    )
    inner_sum = jnp.sum(grad_weights * attn_weights, axis=-1, keepdims=True)
    grad_scores = (attn_weights * (grad_weights - inner_sum)).astype(jnp.bfloat16)
    grad_query = jnp.einsum(
        "nhqk,nkhe->nqhe", grad_scores, key_four, preferred_element_type=jnp.float32
    ).astype(jnp.bfloat16)
    grad_key = jnp.einsum(
        "nhqk,nqhe->nkhe", grad_scores, query_four, preferred_element_type=jnp.float32
    ).astype(jnp.bfloat16)
    grad_value = jnp.einsum(
        "nhqk,nqhe->nkhe",
        attn_weights.astype(jnp.bfloat16),
        grad_four,
        preferred_element_type=jnp.float32,
    ).astype(jnp.bfloat16)
    flat_shape = (number * length, heads_local * HEAD_DIM)
    return (
        grad_query.reshape(flat_shape),
        grad_key.reshape(flat_shape),
        grad_value.reshape(flat_shape),
    )


def layer_forward(weights, stream, allowed):
    gain_pair, shift_pair, w_qkv, bias_qv, w_proj, out_bias, w_up, bias_up, w_down = weights
    number, length, model_width = stream.shape
    flat_rows = stream.reshape(number * length, model_width)
    normed = norm_parts(flat_rows, gain_pair[0], shift_pair[0])[0]
    project = jnp.einsum(
        "rd,dcf->rcf", normed.astype(jnp.bfloat16), w_qkv, preferred_element_type=jnp.float32
    )
    queries = ((project[:, 0] + bias_qv[0]) * HEAD_DIM ** (-0.5)).astype(jnp.bfloat16)
    key_rows = project[:, 1].astype(jnp.bfloat16)
    value_rows = (project[:, 2] + bias_qv[1]).astype(jnp.bfloat16)
    mixture, log_total = attend(queries, key_rows, value_rows, allowed, number, length)
    mixture_low = mixture.astype(jnp.bfloat16)
    attn_part = jnp.dot(mixture_low, w_proj, preferred_element_type=jnp.float32)
    residual = flat_rows + lax.psum(attn_part, "tensor") + out_bias[0]
    normed_two_low = norm_parts(residual, gain_pair[1], shift_pair[1])[0].astype(jnp.bfloat16)
    up_part = jnp.dot(normed_two_low, w_up, preferred_element_type=jnp.float32) + bias_up
    hidden_low = jax.nn.gelu(up_part, approximate=False).astype(jnp.bfloat16)
    down_part = jnp.dot(hidden_low, w_down, preferred_element_type=jnp.float32)
    down_total = lax.psum(down_part.astype(jnp.bfloat16), "tensor").astype(jnp.float32)
    output_low = (residual + down_total + out_bias[1]).astype(jnp.bfloat16)
    kept_parts = (
        queries,
        key_rows,
        value_rows,
        log_total,
        mixture_low,
        residual,
        normed_two_low,
        up_part,
    )
    return (output_low, kept_parts)


def layer_backward(weights, stream, kept_parts, grad_out, allowed):
    gain_pair, shift_pair, w_qkv, bias_qv, w_proj, out_bias, w_up, bias_up, w_down = weights
    queries, key_rows, value_rows, log_total, mixture_low, residual, normed_two_low, up_part = (
        kept_parts
    )
    number, length, model_width = stream.shape
    flat_rows = stream.reshape(number * length, model_width)
    grad_rows = grad_out.reshape(number * length, model_width)
    normed, unit_one, inv_one = norm_parts(flat_rows, gain_pair[0], shift_pair[0])
    normed_low = normed.astype(jnp.bfloat16)
    unit_two, inv_two = norm_parts(residual, gain_pair[1], shift_pair[1])[1:]
    gelu_value, gelu_pull = jax.vjp(partial(jax.nn.gelu, approximate=False), up_part)
    hidden_low = gelu_value.astype(jnp.bfloat16)
    grad_low = grad_rows.astype(jnp.bfloat16)
    grad_down = jnp.einsum("rf,rd->fd", hidden_low, grad_low, preferred_element_type=jnp.float32)
    grad_hidden = jnp.einsum("rd,fd->rf", grad_low, w_down, preferred_element_type=jnp.float32)
    grad_up_rows = gelu_pull(grad_hidden)[0].astype(jnp.bfloat16)
    grad_up = jnp.einsum(
        "rd,rf->df", normed_two_low, grad_up_rows, preferred_element_type=jnp.float32
    )
    grad_bias_up = jnp.sum(grad_up_rows.astype(jnp.float32), axis=0)
    upper_part = jnp.einsum("rf,df->rd", grad_up_rows, w_up, preferred_element_type=jnp.float32)
    grad_normed_two = lax.psum(upper_part, "tensor")
    back_two, grad_gain_two, grad_shift_two = norm_back(
        grad_normed_two, unit_two, inv_two, gain_pair[1]
    )
    grad_residual = grad_rows + back_two
    residual_low = grad_residual.astype(jnp.bfloat16)
    grad_proj = jnp.einsum(
        "rc,rd->cd", mixture_low, residual_low, preferred_element_type=jnp.float32
    )
    grad_mixture = jnp.einsum(
        "rd,cd->rc", residual_low, w_proj, preferred_element_type=jnp.float32
    ).astype(jnp.bfloat16)
    grad_query, grad_key, grad_value = attend_back(
        queries, key_rows, value_rows, log_total, grad_mixture, allowed, number, length
    )
    stacked = jnp.stack([grad_query * HEAD_DIM ** (-0.5), grad_key, grad_value], axis=1)
    grad_qkv = jnp.einsum("rd,rcf->dcf", normed_low, stacked, preferred_element_type=jnp.float32)
    grad_bias_qv = jnp.sum(stacked[:, 0::2].astype(jnp.float32), axis=0)
    lower_part = jnp.einsum("rcf,dcf->rd", stacked, w_qkv, preferred_element_type=jnp.float32)
    grad_normed = lax.psum(lower_part.astype(jnp.bfloat16), "tensor").astype(jnp.float32)
    back_one, grad_gain_one, grad_shift_one = norm_back(
        grad_normed, unit_one, inv_one, gain_pair[0]
    )
    grad_in_low = (grad_residual + back_one).astype(jnp.bfloat16)
    grad_parts = (
        jnp.stack([grad_gain_one, grad_gain_two]),
        jnp.stack([grad_shift_one, grad_shift_two]),
        grad_qkv,
        grad_bias_qv,
        grad_proj,
        jnp.stack([jnp.sum(grad_residual, axis=0), jnp.sum(grad_rows, axis=0)]),
        grad_up,
        grad_bias_up,
        grad_down,
    )
    return (grad_in_low, grad_parts)


def zeros_for(member):
    return jnp.zeros(member.shape, jnp.float32)


def select_member(flag, member):
    return jnp.where(flag, member, jnp.zeros(member.shape, member.dtype))


def masked_tree(flag, tree):
    return jax.tree.map(partial(select_member, flag), tree)


def carry_onward(image_part, text_part):
    return shifted((image_part, text_part), "pipe", 1)


def carry_back(image_part, text_part):
    return shifted((image_part, text_part), "pipe", -1)


def per_device(
    image_side,
    text_side,
    caption_lengths,
    norm_gains,
    norm_shifts,
    w_qkv,
    bias_qv,
    w_proj,
    out_bias,
    w_up,
    bias_up,
    w_down,
):
    weights = (
        norm_gains[0],
        norm_shifts[0],
        w_qkv[0],
        bias_qv[0],
        w_proj[0],
        out_bias[0],
        w_up[0],
        bias_up[0],
        w_down[0],
    )
    is_front = lax.axis_index("pipe") == 0
    is_back = jnp.logical_not(is_front)
    image_local = image_side[0]
    text_local = text_side[0]
    img_each = image_local.shape[0] // MICRO
    txt_each = text_local.shape[0] // MICRO
    image_len = image_local.shape[1]
    text_len = text_local.shape[1]
    model_width = image_local.shape[2]
    image_allow = jnp.ones((img_each, image_len, image_len), jnp.bool_)
    grad_sums = jax.tree.map(zeros_for, weights)

    def local_rows(array_in):
        flat = array_in.reshape(-1, model_width)
        return flat

    front_kept, moved_images, moved_texts = ([], [], [])
    for micro_idx in range(MICRO):
        image_rows = slice(micro_idx * img_each, (micro_idx + 1) * img_each)
        text_rows = slice(micro_idx * txt_each, (micro_idx + 1) * txt_each)
        image_part = image_local[image_rows].astype(jnp.float32)
        image_out, kept_parts = layer_forward(weights, image_part, image_allow)
        front_kept.append(kept_parts)
        moved_image, moved_text = carry_onward(image_out, local_rows(text_local[text_rows]))
        moved_images.append(moved_image)
        moved_texts.append(moved_text)
    text_outs, returned_cots, returned_grads = ([], [], [])
    for micro_idx in range(MICRO):
        image_rows = slice(micro_idx * img_each, (micro_idx + 1) * img_each)
        text_rows = slice(micro_idx * txt_each, (micro_idx + 1) * txt_each)
        text_cot = text_local[text_rows].astype(jnp.float32)
        text_allow = caption_mask(caption_lengths[text_rows], text_len)
        text_in = (
            moved_texts[micro_idx].reshape(txt_each, text_len, model_width).astype(jnp.float32)
        )
        text_out, kept_parts = layer_forward(weights, text_in, text_allow)
        text_grad, grad_parts = layer_backward(weights, text_in, kept_parts, text_cot, text_allow)
        grad_sums = jax.tree.map(jnp.add, grad_sums, masked_tree(is_back, grad_parts))
        text_outs.append(text_out)
        returned_cot, returned_grad = carry_back(local_rows(image_local[image_rows]), text_grad)
        returned_cots.append(returned_cot)
        returned_grads.append(returned_grad)
    image_grads = []
    for micro_idx in range(MICRO):
        image_rows = slice(micro_idx * img_each, (micro_idx + 1) * img_each)
        image_part = image_local[image_rows].astype(jnp.float32)
        kept_parts = front_kept[micro_idx]
        image_cot = (
            returned_cots[micro_idx].reshape(img_each, image_len, model_width).astype(jnp.float32)
        )
        image_grad, grad_parts = layer_backward(
            weights, image_part, kept_parts, image_cot, image_allow
        )
        grad_sums = jax.tree.map(jnp.add, grad_sums, masked_tree(is_front, grad_parts))
        image_grads.append(image_grad)
    image_grad_all, text_out_all = (jnp.stack(image_grads), jnp.stack(text_outs))
    image_shape = (MICRO * img_each, image_len, model_width)
    image_result = jnp.where(
        is_front, image_grad_all.reshape(image_shape), jnp.stack(moved_images).reshape(image_shape)
    )[None]
    text_result = jnp.where(is_front, jnp.stack(returned_grads), text_out_all)[None]
    matrix_grads = (
        lax.psum_scatter(
            grad_sums[2].astype(jnp.bfloat16), "dp", scatter_dimension=0, tiled=True
        ).astype(jnp.float32),
        lax.psum_scatter(
            grad_sums[4].astype(jnp.bfloat16), "dp", scatter_dimension=1, tiled=True
        ).astype(jnp.float32),
        lax.psum_scatter(
            grad_sums[6].astype(jnp.bfloat16), "dp", scatter_dimension=0, tiled=True
        ).astype(jnp.float32),
        lax.psum_scatter(
            grad_sums[8].astype(jnp.bfloat16), "dp", scatter_dimension=1, tiled=True
        ).astype(jnp.float32),
    )
    vector_grads = lax.psum(
        (grad_sums[0], grad_sums[1], grad_sums[3], grad_sums[5], grad_sums[7]), "dp"
    )
    return (
        image_result,
        text_result,
        vector_grads[0][None],
        vector_grads[1][None],
        matrix_grads[0][None],
        vector_grads[2][None],
        matrix_grads[1][None],
        vector_grads[3][None],
        matrix_grads[2][None],
        vector_grads[4][None],
        matrix_grads[3][None],
    )


def solution(mesh):
    placed = (
        P("pipe", "dp", None, None),
        P("pipe", "dp", None, None),
        P("dp", None),
        P("pipe", None, None),
        P("pipe", None, None),
        P("pipe", None, None, "tensor"),
        P("pipe", None, "tensor"),
        P("pipe", "tensor", None),
        P("pipe", None, None),
        P("pipe", None, "tensor"),
        P("pipe", "tensor"),
        P("pipe", "tensor", None),
    )
    return jax.shard_map(
        per_device,
        mesh=mesh,
        in_specs=placed,
        out_specs=(
            P("pipe", "dp", None, None),
            P("pipe", "dp", None, None),
            P("pipe", None, None),
            P("pipe", None, None),
            P("pipe", "dp", None, "tensor"),
            P("pipe", None, "tensor"),
            P("pipe", "tensor", "dp"),
            P("pipe", None, None),
            P("pipe", "dp", "tensor"),
            P("pipe", "tensor"),
            P("pipe", "tensor", "dp"),
        ),
        check_vma=False,
    )
```

profile of v0, /device:TPU:0, one launch (start us, length us, event | category | flops | bytes accessed | tf_op | source)
XLA Modules:
  0.0 824.7 jit_solution(16801588300543937478)
XLA Ops:
  10.1 4.9 collective-permute-start.6
  16.9 3.1 fusion.52
  22.1 3.3 fusion.55
  66.7 3.2 fusion.240
  84.6 4.4 fusion.310
  100.5 132.8 %all-reduce.10.cloned.1.call-done = (f32[788,768]{1,0:T(8,128)}, f32[788,768]{1,0:T(8,128)}, f32[512,768]{1,0:T(8,128)}, f32[512,768]{1,0:T(8,128)}) async-done(((f32[788,768]{1,0:T(8,128)}, f32[788,768]{1,0:T(8,128)}, f32[512,768]{1,0:T(8,128)}, f32[512,768]{1,0:T(8,128)}), (f32[788,768]{1,0:T(8,128)}, f32[788,768]{1,0:T(8,128)}, f32[512,768]{1,0:T(8,128)}, ...) | async-done | bytes 7987216 | tf_op jit(solution)/shard_map/psum | solution.py:120
  233.4 3.5 fusion.306
  240.4 14.0 %multiply_convert_fusion.5 = (bf16[788,768]{1,0:T(8,128)(2,1)}, f32[788,768]{1,0:T(8,128)S(1)}, bf16[788,768]{1,0:T(8,128)(2,1)}, f32[788,768]{1,0:T(8,128)S(1)}, f32[788,768]{1,0:T(8,128)S(1)}) fusion(f32[768]{0:T(1024)S(1)} %reduce.29, f32[788,768]{1,0:T(8,128)S(1)} %fusion.182, bf16[1,768,768]{2,1,0:T(8,128)(2,1)S(1)} %copy-done, ...), kind=kOutput, calls=%fused_computation.90 | convolution fusion | flops 1012472832 | bytes 15719584 | tf_op jit(solution)/shard_map/dot_general | solution.py:122
  254.4 3.7 convert_reduce_fusion.6
  260.7 3.7 convert_reduce_fusion.7
  269.0 5.0 multiply_convert_fusion.6
  278.2 5.5 multiply_convert_fusion.7
  300.2 3.1 add_convert_fusion.6
  306.2 3.9 convolution_convert_fusion
  318.9 118.0 %all-reduce.8.cloned.1.call-done = (f32[788,768]{1,0:T(8,128)}, f32[788,768]{1,0:T(8,128)}, f32[512,768]{1,0:T(8,128)}, f32[512,768]{1,0:T(8,128)}) async-done(((f32[788,768]{1,0:T(8,128)}, f32[788,768]{1,0:T(8,128)}, f32[512,768]{1,0:T(8,128)}, f32[512,768]{1,0:T(8,128)}), (f32[788,768]{1,0:T(8,128)}, f32[788,768]{1,0:T(8,128)}, f32[512,768]{1,0:T(8,128)}, ...) | async-done | bytes 7987216 | tf_op jit(solution)/shard_map/psum | solution.py:162
  437.0 5.8 multiply_reduce_fusion.5
  442.8 5.7 fusion.297
  476.2 3.4 convert_reduce_fusion.13
  509.3 3.6 multiply_reduce_fusion
  525.2 3.3 multiply_reduce_fusion.1
  537.5 3.6 fusion.124
  547.0 3.3 convolution_convert_fusion.2
  592.1 148.4 %all-reduce.12.cloned.1.call-done = (bf16[788,768]{1,0:T(8,128)(2,1)}, bf16[788,768]{1,0:T(8,128)(2,1)}, bf16[788,768]{1,0:T(8,128)(2,1)}, bf16[788,768]{1,0:T(8...) async-done(((bf16[788,768]{1,0:T(8,128)(2,1)}, bf16[788,768]{1,0:T(8,128)(2,1)}, ...) | async-done | bytes 7987216 | tf_op jit(solution)/shard_map/psum | solution.py:181
  740.5 3.0 fusion.35
  743.6 5.5 fusion.37
  751.4 4.6 collective-permute-start.3
  766.2 19.6 %all-reduce.2 = (f32[1,2,768]{2,1,0:T(2,128)}, f32[1,2,768]{2,1,0:T(2,128)}, f32[1,2,192]{2,1,0:T(2,128)}, f32[1,2,768]{2,1,0:T(2,128)}, f32[1,768]{1,0:T(1,128)}) all-reduce(f32[1,2,768]{2,1,0:T(2,128)S(1)} %fusion.268, f32[1,2,768]{2,1,0:T(2,128)S(1)} %fusion.267, ...), channel_id=1, replica_groups=mesh['pipe'=2,'dp'=4,'tensor'=4] {'dp'}, use_global_device_ids=true, to_apply=%region_72.73 | all-reduce | flops 5760 | bytes 46080 | tf_op jit(solution)/shard_map/psum | solution.py:320
  789.8 11.8 %collective-permute-done.5 = bf16[512,768]{1,0:T(8,128)(2,1)} collective-permute-done((bf16[512,768]{1,0:T(8,128)(2,1)}, bf16[512,768]{1,0:T(8,128)(2,1)}, u32[]{:S(2)}, u32[]{:S(2)}) %collective-permute-start.5) | collective-permute-done | bytes 786464 | tf_op jit(solution)/shard_map/ppermute | solution.py:19
  804.4 3.0 collective-permute-done.2
  807.4 3.5 maximum_select_fusion
  810.9 3.1 select_n.241
  814.1 3.6 copy.271
  (747 shorter events, 260.7 us)
Async XLA Ops:
  7.2 231.8 %copy-start = (bf16[1,768,768]{2,1,0:T(8,128)(2,1)S(1)}, bf16[1,768,768]{2,1,0:T(8,128)(2,1)}, u32[]{:S(2)}) copy-start(bf16[1,768,768]{2,1,0:T(8,128)(2,1)} %param.21) | copy-start | bytes 3538948
  7.2 226.2 %all-reduce.10.cloned.1.call-start = ((), (), s32[]{:S(2)}) async-start(), calls=%async_computation.9 | async-start | bytes 16023552 | tf_op jit(solution)/shard_map/psum | solution.py:120
  10.1 61.8 %collective-permute-start.6 = (bf16[512,768]{1,0:T(8,128)(2,1)}, bf16[512,768]{1,0:T(8,128)(2,1)S(1)}, u32[]{:S(2)}, u32[]{:S(2)}) collective-permute-start(bf16[512,768]{1,0:T(8,128)(2,1)} %get-tuple-element.170), channel_id=1, source_target_pairs={{0,16},{1,17},{2,18},{3,19},{4,20},{5,21},{6,22},{7,23},{8,24},{9,... | collective-permute-start | bytes 2359304 | tf_op jit(solution)/shard_map/ppermute | solution.py:19
  14.9 58.9 %collective-permute-start.4 = (bf16[512,768]{1,0:T(8,128)(2,1)}, bf16[512,768]{1,0:T(8,128)(2,1)S(1)}, u32[]{:S(2)}, u32[]{:S(2)}) collective-permute-start(bf16[512,768]{1,0:T(8,128)(2,1)} %get-tuple-element.169), channel_id=1, source_target_pairs={{0,16},{1,17},{2,18},{3,19},{4,20},{5,21},{6,22},{7,23},{8,24},{9,... | collective-permute-start | bytes 2359304 | tf_op jit(solution)/shard_map/ppermute | solution.py:19
  22.1 52.3 %copy-start.128 = (f32[768]{0:T(1024)}, f32[768]{0:T(1024)S(1)}, u32[]{:S(2)}) copy-start(f32[768]{0:T(1024)S(1)} %get-tuple-element.231) | copy-start | bytes 9220
  22.1 256.1 %copy-start.138 = (f32[768]{0:T(1024)}, f32[768]{0:T(1024)S(1)}, u32[]{:S(2)}) copy-start(f32[768]{0:T(1024)S(1)} %get-tuple-element.232) | copy-start | bytes 9220
  45.6 33.9 %copy-start.136 = (f32[3,64]{1,0:T(4,128)}, f32[3,64]{1,0:T(4,128)S(1)}, u32[]{:S(2)}) copy-start(f32[3,64]{1,0:T(4,128)S(1)} %add.548) | copy-start | bytes 2308
  49.0 31.8 %copy-start.163 = (f32[3,64]{1,0:T(4,128)}, f32[3,64]{1,0:T(4,128)S(1)}, u32[]{:S(2)}) copy-start(f32[3,64]{1,0:T(4,128)S(1)} %add.545) | copy-start | bytes 2308
  71.8 195.2 %copy-start.34 = (bf16[512,768]{1,0:T(8,128)(2,1)}, bf16[512,768]{1,0:T(8,128)(2,1)S(1)}, u32[]{:S(2)}) copy-start(bf16[512,768]{1,0:T(8,128)(2,1)S(1)} %collective-permute-done.6) | copy-start | bytes 2359300
  84.5 352.4 %all-reduce.8.cloned.1.call-start = ((), (), s32[]{:S(2)}) async-start(), calls=%async_computation.8 | async-start | bytes 16023552 | tf_op jit(solution)/shard_map/psum | solution.py:162
  92.0 144.9 %copy-start.41 = (bf16[788,768]{1,0:T(8,128)(2,1)}, bf16[788,768]{1,0:T(8,128)(2,1)S(1)}, u32[]{:S(2)}) copy-start(bf16[788,768]{1,0:T(8,128)(2,1)S(1)} %reshape.1018) | copy-start | bytes 3631108
  92.0 162.3 %collective-permute-start.1 = (bf16[788,768]{1,0:T(8,128)(2,1)S(1)}, bf16[788,768]{1,0:T(8,128)(2,1)}, u32[]{:S(2)}, u32[]{:S(2)}) collective-permute-start(bf16[788,768]{1,0:T(8,128)(2,1)S(1)} %reshape.1018), channel_id=1, source_target_pairs={{16,0},{17,1},{18,2},{19,3},{20,4},{21,5},{22,6},{23,7},{24,8},{25... | collective-permute-start | bytes 3631112 | tf_op jit(solution)/shard_map/ppermute | solution.py:19
  98.6 162.1 %collective-permute-start = (bf16[788,768]{1,0:T(8,128)(2,1)}, bf16[788,768]{1,0:T(8,128)(2,1)}, u32[]{:S(2)}, u32[]{:S(2)}) collective-permute-start(bf16[788,768]{1,0:T(8,128)(2,1)} %reshape.1016), channel_id=1, source_target_pairs={{16,0},{17,1},{18,2},{19,3},{20,4},{21,5},{22,6},{23,7},{24,8},{25... | collective-permute-start | bytes 3631112 | tf_op jit(solution)/shard_map/ppermute | solution.py:19
  99.9 160.8 %copy-start.219 = (f32[768]{0:T(1024)}, f32[768]{0:T(1024)S(1)}, u32[]{:S(2)}) copy-start(f32[768]{0:T(1024)S(1)} %reduce.29) | copy-start | bytes 9220
  268.3 41.8 %copy-start.21 = (f32[512,768]{1,0:T(8,128)}, f32[512,768]{1,0:T(8,128)S(1)}, u32[]{:S(2)}) copy-start(f32[512,768]{1,0:T(8,128)S(1)} %get-tuple-element.148) | copy-start | bytes 4718596
  288.4 275.0 %reduce-scatter.15.cloned.1.call-start = ((), (), s32[]{:S(2)}) async-start(), calls=%async_computation.7 | async-start | bytes 1474560
  304.8 262.9 %reduce-scatter.11.cloned.1.call-start = ((), (), s32[]{:S(2)}) async-start(), calls=%async_computation.5 | async-start | bytes 1474560 | tf_op jit(solution)/shard_map/reduce_scatter | solution.py:313
  316.2 120.7 %copy-start.140 = (f32[768]{0:T(1024)S(1)}, f32[768]{0:T(1024)}, u32[]{:S(2)}) copy-start(f32[768]{0:T(1024)} %copy-done.138) | copy-start | bytes 9220
  316.2 120.7 %copy-start.153 = (f32[788]{0:T(1024)S(1)}, f32[788]{0:T(1024)}, u32[]{:S(2)}) copy-start(f32[788]{0:T(1024)} %copy-done.151) | copy-start | bytes 9460
  316.2 120.7 %copy-start.172 = (f32[788]{0:T(1024)S(1)}, f32[788]{0:T(1024)}, u32[]{:S(2)}) copy-start(f32[788]{0:T(1024)} %copy-done.170) | copy-start | bytes 9460
  318.7 269.8 %reduce-scatter.13.cloned.1.call-start = ((), (), s32[]{:S(2)}) async-start(), calls=%async_computation.6 | async-start | bytes 491520
  537.4 52.9 %reduce-scatter.9.cloned.1.call-start = ((), (), s32[]{:S(2)}) async-start(), calls=%async_computation.4 | async-start | bytes 1474560 | tf_op jit(solution)/shard_map/reduce_scatter | solution.py:307
  546.9 193.6 %all-reduce.12.cloned.1.call-start = ((), (), s32[]{:S(2)}) async-start(), calls=%async_computation.10 | async-start | bytes 16023552 | tf_op jit(solution)/shard_map/psum | solution.py:181
  565.5 20.3 %copy-start.116 = (bf16[3,64,512]{2,1,0:T(8,128)(2,1)S(1)}, bf16[3,64,512]{2,1,0:T(8,128)(2,1)}, u32[]{:S(2)}) copy-start(bf16[3,64,512]{2,1,0:T(8,128)(2,1)} %convolution_convert_fusion.14) | copy-start | bytes 589828
  565.5 21.5 %copy-start.114 = (bf16[3,64,512]{2,1,0:T(8,128)(2,1)S(1)}, bf16[3,64,512]{2,1,0:T(8,128)(2,1)}, u32[]{:S(2)}) copy-start(bf16[3,64,512]{2,1,0:T(8,128)(2,1)} %convolution_convert_fusion.16) | copy-start | bytes 589828
  567.8 19.3 %copy-start.125 = (bf16[3,64,512]{2,1,0:T(8,128)(2,1)S(1)}, bf16[3,64,512]{2,1,0:T(8,128)(2,1)}, u32[]{:S(2)}) copy-start(bf16[3,64,512]{2,1,0:T(8,128)(2,1)} %fusion.196) | copy-start | bytes 589828
  567.8 19.3 %copy-start.135 = (bf16[3,64,512]{2,1,0:T(8,128)(2,1)S(1)}, bf16[3,64,512]{2,1,0:T(8,128)(2,1)}, u32[]{:S(2)}) copy-start(bf16[3,64,512]{2,1,0:T(8,128)(2,1)} %fusion.190) | copy-start | bytes 589828
  587.3 153.2 %copy-start.169 = (f32[788]{0:T(1024)S(1)}, f32[788]{0:T(1024)}, u32[]{:S(2)}) copy-start(f32[788]{0:T(1024)} %rsqrt.82) | copy-start | bytes 9460
  751.4 53.0 %collective-permute-start.3 = (bf16[788,768]{1,0:T(8,128)(2,1)}, bf16[788,768]{1,0:T(8,128)(2,1)}, u32[]{:S(2)}, u32[]{:S(2)}) collective-permute-start(bf16[788,768]{1,0:T(8,128)(2,1)} %get-tuple-element.184), channel_id=1, source_target_pairs={{0,16},{1,17},{2,18},{3,19},{4,20},{5,21},{6,22},{7,23},{8,24},{9,... | collective-permute-start | bytes 3631112 | tf_op jit(solution)/shard_map/ppermute | solution.py:19
  756.0 51.4 %collective-permute-start.2 = (bf16[788,768]{1,0:T(8,128)(2,1)}, bf16[788,768]{1,0:T(8,128)(2,1)}, u32[]{:S(2)}, u32[]{:S(2)}) collective-permute-start(bf16[788,768]{1,0:T(8,128)(2,1)} %get-tuple-element.183), channel_id=1, source_target_pairs={{0,16},{1,17},{2,18},{3,19},{4,20},{5,21},{6,22},{7,23},{8,24},{9,... | collective-permute-start | bytes 3631112 | tf_op jit(solution)/shard_map/ppermute | solution.py:19
  763.4 26.4 %collective-permute-start.7 = (bf16[512,768]{1,0:T(8,128)(2,1)}, bf16[512,768]{1,0:T(8,128)(2,1)}, u32[]{:S(2)}, u32[]{:S(2)}) collective-permute-start(bf16[512,768]{1,0:T(8,128)(2,1)} %fusion.81), channel_id=1, source_target_pairs={{16,0},{17,1},{18,2},{19,3},{20,4},{21,5},{22,6},{23,7},{24,8},{25... | collective-permute-start | bytes 2359304 | tf_op jit(solution)/shard_map/ppermute | solution.py:19
  764.7 36.9 %collective-permute-start.5 = (bf16[512,768]{1,0:T(8,128)(2,1)}, bf16[512,768]{1,0:T(8,128)(2,1)}, u32[]{:S(2)}, u32[]{:S(2)}) collective-permute-start(bf16[512,768]{1,0:T(8,128)(2,1)} %get-tuple-element.182), channel_id=1, source_target_pairs={{16,0},{17,1},{18,2},{19,3},{20,4},{21,5},{22,6},{23,7},{24,8},{25... | collective-permute-start | bytes 2359304 | tf_op jit(solution)/shard_map/ppermute | solution.py:19
  (224 other events, 734.1 us)
Sparse Core Ops, SparseCore 0:
  84.6 148.6 all-reduce.9
  288.5 148.3 all-reduce.7
  439.2 29.1 reduce-scatter.14
  470.6 27.8 reduce-scatter.10
  537.5 20.5 reduce-scatter.12
  560.4 27.4 reduce-scatter.8
  592.0 148.4 all-reduce.11
where the time goes:
time: 832 us; the launch traced here: 825 us
  waiting for transfers between devices  414 us (50%)
  matrix products  150 us (18%)
  local copies, waits for them, and re-layouts  131 us (16%)
  other arithmetic  73.4 us (9%)
  blocking collectives  19.6 us (2%)
  starting transfers between devices  18.9 us (2%)
  between operations  17.2 us (2%)
    psum x1, waiting for transfers between devices, layer_backward(): lax.psum(lower_part.astype(jnp.bfloat16), 'tensor').astype(jnp.float32)  148 us
    psum x1, waiting for transfers between devices, layer_forward(): residual = flat_rows + lax.psum(attn_part, 'tensor') + out_bias[0]  133 us
    psum x1, waiting for transfers between devices, layer_backward(): grad_normed_two = lax.psum(upper_part, 'tensor')  118 us
    unnamed x496, local copies, waits for them, and re-layouts  37.1 us
    dot_general x4, matrix products, layer_forward(): jnp.dot(normed_two_low, w_up, preferred_element_type=jnp.float32) + bias_up  25.8 us
    reduce_sum x6, other arithmetic, norm_back(): jnp.sum(grad_out * unit_rows, axis=0)  19.6 us
    psum x1, blocking collectives, per_device(): lax.psum((grad_sums[0], grad_sums[1], grad_sums[3], grad_sums[5], grad_su...  19.6 us
    ppermute x8, starting transfers between devices, shifted(): return lax.ppermute(block, axis, route)  18.5 us
  transfers between devices with their start and end apart: 15, of which 5 were waited for; matrix products, arithmetic and copies ran while one was open for 34% of the time, Pallas kernels for 0%

commit v1 on v0

v1 whole, which is shorter than its diff:
```python
from functools import partial

import jax
import jax.numpy as jnp
from jax import lax
from jax.experimental import pallas as pl
from jax.experimental.pallas import tpu as pltpu
from jax.sharding import PartitionSpec as P

F32 = jnp.float32
BF16 = jnp.bfloat16
BY_MESH = pl.DeviceIdType.MESH
HEAD = 64
HALF = 3
HEADS = 2 * HALF
WIDE = HALF * HEAD
EPSILON = 1e-06
MASKED = -1000000000.0
CHUNKS = 4
STRIP = 16
QKV = 640
MIX = 256
TILE = 256

K_IN, K_A, K_B, K_C, K_Y1, K_Y2, K_YT, K_OI, K_OT, K_T1, K_T2, K_W, K_S, K_G, K_Z = range(15)
N_KINDS = K_Z + 5


def dot(a, b):
    return lax.dot_general(a, b, (((1,), (0,)), ((), ())), preferred_element_type=F32)


def dot_nt(a, b):
    return lax.dot_general(a, b, (((1,), (1,)), ((), ())), preferred_element_type=F32)


def dot_tn(a, b):
    return lax.dot_general(a, b, (((0,), (0,)), ((), ())), preferred_element_type=F32)


def loop(count, body):
    def step(j, carry):
        body(j)
        return carry

    lax.fori_loop(0, count, step, 0)


def unit_of(rows):
    centre = rows - jnp.mean(rows, axis=-1, keepdims=True)
    inverse = lax.rsqrt(jnp.mean(centre * centre, axis=-1, keepdims=True) + EPSILON)
    return centre * inverse, inverse


def norm_back(grad, unit, inverse, gain):
    scaled = grad * gain
    first = jnp.mean(scaled, axis=-1, keepdims=True)
    second = jnp.mean(scaled * unit, axis=-1, keepdims=True)
    return inverse * (scaled - first - unit * second)


def gelu_pair(u):
    cdf = 0.5 * (1.0 + lax.erf(u * (0.5**0.5)))
    pdf = jnp.exp(u * u * -0.5) * 0.3989422804014327
    return u * cdf, cdf + u * pdf


def fold(rows):
    return jnp.sum(rows.reshape(rows.shape[0] // 8, 8, rows.shape[1]), axis=0)


def layers_kernel(
    rows_i, rows_t, keys_i, dp_size, z_inside,
    img_own, txt_own, w_qkv, w_proj, w_up, w_down, small, gains, shifts, outb, seg_col, seg_row,
    img_out, txt_out, g_qkv, g_proj, g_up, g_down, vec_out,
    x_s, dy_s, wq_s, wp_s, wu_s, wd_s, small_s, a1_s, qkv_s, o_s, r_s, a2_s, gb_s, du_s, p_s, dkv_s, do_s,
    send_s, ra_s, rb_s, rc_s, ys_s, yt_s, y1_s, y2_s, fin_s, acc_s, vec_s, vrec_s, vall_s,
    gs_q, gs_p, gs_u, gs_d, gr_q, gr_p, gr_u, gr_d, *rest,
):
    if z_inside:
        zr_q, zr_p, zr_u, zr_d, zf_q, zf_p, zf_u, zf_d, ssem, rsem, lsem = rest
    else:
        ssem, rsem, lsem = rest
    width = x_s.shape[1]
    p, d, t = lax.axis_index("pipe"), lax.axis_index("dp"), lax.axis_index("tensor")
    core = lax.rem(t, 2)
    sib_t = t + 1 - 2 * core
    peer_t = lax.rem(t + 2, 4)
    other = 1 - p
    sib, peer = (p, d, sib_t), (p, d, peer_t)
    across, across_peer, across_sib = (other, d, t), (other, d, peer_t), (other, d, sib_t)
    offsets = range(1, dp_size) if z_inside else range(0)
    partners = [sib, peer, across, across_peer, across_sib]
    partners += [(p, lax.rem(d + k, dp_size), t) for k in offsets]

    def remote(src, dst, kind, slot, to):
        at = kind * 4 + slot
        return pltpu.make_async_remote_copy(
            src_ref=src, dst_ref=dst, send_sem=ssem.at[at], recv_sem=rsem.at[at],
            device_id=to, device_id_type=BY_MESH,
        )

    def local(src, dst, slot):
        return pltpu.make_async_copy(src, dst, lsem.at[slot])

    image_here = p == 0
    n_img = rows_i * CHUNKS
    n_txt = rows_t * CHUNKS

    wq_own = local(w_qkv, wq_s.at[:, 0:QKV], 0)
    wp_own = local(w_proj, wp_s.at[0:WIDE], 1)
    wu_own = local(w_up, wu_s.at[:, 0:width], 2)
    wd_own = local(w_down, wd_s.at[0:width], 3)
    sm_own = local(small, small_s.at[0], 4)
    img_in = local(img_own, x_s, 5)
    txt_in = local(txt_own, dy_s.at[0:n_txt], 6)
    sm_own.start()
    wq_own.start()

    @pl.when(image_here)
    def _():
        img_in.start()

    @pl.when(jnp.logical_not(image_here))
    def _():
        txt_in.start()

    wp_own.start()
    wu_own.start()
    wd_own.start()
    zero_rows = jnp.zeros((MIX - WIDE, width), BF16)
    wp_s[WIDE:MIX, :] = zero_rows
    wp_s[MIX + WIDE :, :] = zero_rows
    acc_s[...] = jnp.zeros_like(acc_s)

    barrier = pltpu.get_barrier_semaphore()
    for to in partners:
        pl.semaphore_signal(barrier, inc=1, device_id=to, device_id_type=BY_MESH)
    pl.semaphore_wait(barrier, len(partners))

    sm_sib = remote(small, small_s.at[1], K_S, 0, sib)
    wq_sib = remote(w_qkv, wq_s.at[:, QKV:], K_W, 0, sib)
    wp_sib = remote(w_proj, wp_s.at[MIX : MIX + WIDE], K_W, 1, sib)
    wu_sib = remote(w_up, wu_s.at[:, width:], K_W, 2, sib)
    wd_sib = remote(w_down, wd_s.at[width:], K_W, 3, sib)

    def x_to_text(i):
        rows = pl.ds(pl.multiple_of(i * rows_t, 16), rows_t)
        return remote(txt_own.at[rows], x_s.at[rows], K_IN, i, across)

    def dy_to_image(i):
        rows = pl.ds(pl.multiple_of(i * rows_i, 16), rows_i)
        return remote(img_own.at[rows], dy_s.at[rows], K_IN, i, across)

    @pl.when(image_here)
    def _():
        loop(CHUNKS, lambda i: x_to_text(i).start())

    sm_sib.start()
    wq_sib.start()

    @pl.when(jnp.logical_not(image_here))
    def _():
        loop(CHUNKS, lambda i: dy_to_image(i).start())

    wp_sib.start()
    wu_sib.start()
    wd_sib.start()

    own_gain = [gains[0:1, :], gains[1:2, :]]
    own_shift = [shifts[0:1, :], shifts[1:2, :]]

    g_arrays = [(gs_q, gr_q), (gs_p, gr_p), (gs_u, gr_u), (gs_d, gr_d)]

    def g_exchange(a):
        return remote(g_arrays[a][0], g_arrays[a][1], K_G, a, sib)

    def grads_pair(a, left, right, n, own_cols, sib_cols):
        mine, theirs = g_arrays[a]
        tiles = width // TILE

        def part(cols):
            def body(m):
                at = pl.ds(pl.multiple_of(m * TILE, TILE), TILE)
                return at, dot_tn(left[0:n, at], right[0:n, cols[0] : cols[1]])

            return body

        first, second = part(sib_cols), part(own_cols)

        def send_half(m):
            at, value = first(m)
            mine[at, :] = value.astype(BF16)

        loop(tiles, send_half)
        g_exchange(a).start()

        def finish():
            g_exchange(a).wait()

            def own_half(m):
                at, value = second(m)
                mine[at, :] = (value + theirs[at, :].astype(F32)).astype(BF16)

            loop(tiles, own_half)

        return finish

    z_sets = [(gs_q, zr_q, zf_q, g_qkv), (gs_p, zr_p, zf_p, g_proj), (gs_u, zr_u, zf_u, g_up), (gs_d, zr_d, zf_d, g_down)] if z_inside else []
    share = width // dp_size

    def z_copy(a, k):
        whole, landing = z_sets[a][0:2]
        to = lax.rem(d + k, dp_size)
        rows = pl.ds(pl.multiple_of(to * share, 16), share)
        return remote(whole.at[rows], landing.at[k - 1], K_Z + a, k - 1, (p, to, t))

    out_plain = [(gs_q, g_qkv), (gs_p, g_proj), (gs_u, g_up), (gs_d, g_down)]

    def z_start(a):
        if z_inside:
            for k in offsets:
                z_copy(a, k).start()
        else:
            local(out_plain[a][0], out_plain[a][1], 20 + a).start()

    def z_finish(a):
        if z_inside:
            whole, landing, final, result = z_sets[a]
            for k in offsets:
                z_copy(a, k).wait()

            def body(j):
                at = pl.ds(pl.multiple_of(j * STRIP, STRIP), STRIP)
                rows = pl.ds(pl.multiple_of(d * share + j * STRIP, STRIP), STRIP)
                total = whole[rows, :].astype(F32)
                for k in offsets:
                    total = total + landing[k - 1, at, :].astype(F32)
                final[at, :] = total

            loop(share // STRIP, body)
            local(final, result, 20 + a).start()

    def z_end(a):
        if z_inside:
            local(z_sets[a][2], z_sets[a][3], 20 + a).wait()
        else:
            local(out_plain[a][0], out_plain[a][1], 20 + a).wait()

    def one_layer(text):
        rows = rows_t if text else rows_i
        total = rows * CHUNKS
        strips = rows // STRIP
        q_off = rows_t if text else 0

        def at_rows(i):
            return pl.ds(pl.multiple_of(i * rows, 16), rows)

        def q_rows(i):
            return pl.ds(pl.multiple_of(i * rows + q_off, 16), rows)

        def strip_rows(i, j):
            return pl.ds(pl.multiple_of(i * rows + j * STRIP, STRIP), STRIP)

        def swap(i, landing, kind):
            return remote(send_s.at[at_rows(i)], landing.at[at_rows(i)], kind, i, peer)

        incoming = dy_to_image if not text else x_to_text

        def wait_input(i):
            cp = remote(x_s.at[at_rows(i)] if text else dy_s.at[at_rows(i)],
                        x_s.at[at_rows(i)] if text else dy_s.at[at_rows(i)], K_IN, i, across)
            cp.wait_recv()

        wq_own.wait()
        wq_sib.wait()
        sm_own.wait()
        sm_sib.wait()
        if text:
            txt_in.wait()
            pad = jnp.zeros((rows_t, 2 * QKV), BF16)
            qkv_s[0:rows_t, :] = pad
            qkv_s[rows_t + total : 2 * rows_t + total, :] = pad
            dkv_s[...] = jnp.zeros_like(dkv_s)
        else:
            img_in.wait()
        for s in range(2):
            o_s[0:total, s * MIX + WIDE : (s + 1) * MIX] = jnp.zeros((total, MIX - WIDE), BF16)

        def project(i):
            if text:
                wait_input(i)

            def first_norm(j):
                at = strip_rows(i, j)
                unit, _ = unit_of(x_s[at, :].astype(F32))
                a1_s[at, :] = (unit * own_gain[0] + own_shift[0]).astype(BF16)

            loop(strips, first_norm)
            left = a1_s[at_rows(i), :]
            lanes = lax.broadcasted_iota(jnp.int32, (1, QKV), 1)
            factor = jnp.where(lanes < WIDE, HEAD**-0.5, 1.0).astype(F32)
            for s in range(2):
                value = dot(left, wq_s[:, s * QKV : (s + 1) * QKV])
                value = (value + small_s[s, 0:1, width : width + QKV]) * factor
                qkv_s[q_rows(i), s * QKV : (s + 1) * QKV] = value.astype(BF16)

        def head_at(h):
            s, hh = h // HALF, h % HALF
            base = s * QKV + hh * HEAD
            return slice(base, base + HEAD), slice(base + WIDE, base + WIDE + HEAD), slice(base + 2 * WIDE, base + 2 * WIDE + HEAD), slice(s * MIX + hh * HEAD, s * MIX + hh * HEAD + HEAD)

        span = 3 * rows_t if text else rows_i

        def key_rows(i):
            return pl.ds(pl.multiple_of(i * rows, 16), span)

        def allowed(i):
            if text:
                mine = seg_col[at_rows(i), 0:1]
                keys = seg_row[0:1, pl.ds(pl.multiple_of(i * rows_t, 128), span)]
                return mine == keys
            return lax.broadcasted_iota(jnp.int32, (1, span), 1) < keys_i

        def attend(i):
            ok = allowed(i)
            for h in range(HEADS):
                qc, kc, vc, oc = head_at(h)
                scores = dot_nt(qkv_s[q_rows(i), qc], qkv_s[key_rows(i), kc])
                scores = jnp.where(ok, scores, MASKED)
                raised = jnp.exp(scores - jnp.max(scores, axis=-1, keepdims=True))
                weights = raised * (1.0 / jnp.sum(raised, axis=-1, keepdims=True))
                p_s[i * HEADS + h, 0:rows, 0:span] = weights
                mixed = dot(weights.astype(BF16), qkv_s[key_rows(i), vc])
                o_s[at_rows(i), oc] = mixed.astype(BF16)

        def send_a(i):
            send_s[at_rows(i), :] = dot(o_s[at_rows(i), :], wp_s[...]).astype(BF16)
            swap(i, ra_s, K_A).start()

        if text:
            loop(CHUNKS, project)
            wp_own.wait()
            wp_sib.wait()

            def forward(i):
                attend(i)
                send_a(i)

            loop(CHUNKS, forward)
        else:

            def forward(i):
                project(i)
                attend(i)

                @pl.when(i == 0)
                def _():
                    wp_own.wait()
                    wp_sib.wait()

                send_a(i)

            loop(CHUNKS, forward)
        wu_own.wait()
        wu_sib.wait()
        wd_own.wait()
        wd_sib.wait()

        def y_copies(i):
            at = at_rows(i)
            if text:
                return [remote(ys_s.at[at], yt_s.at[at], K_YT, i, peer)]
            return [
                remote(ys_s.at[at], y1_s.at[at], K_Y1, i, across),
                remote(ys_s.at[at], y2_s.at[at], K_Y2, i, across_peer),
            ]

        def middle(i):
            if not text:
                wait_input(i)
            swap(i, ra_s, K_A).wait()

            def second_norm(j):
                at = strip_rows(i, j)
                r = x_s[at, :].astype(F32) + (send_s[at, :].astype(F32) + ra_s[at, :].astype(F32)) + outb[0:1, :]
                r_s[at, :] = r
                unit, _ = unit_of(r)
                a2_s[at, :] = (unit * own_gain[1] + own_shift[1]).astype(BF16)
                acc_s[5] += fold(dy_s[at, :].astype(F32))

            loop(strips, second_norm)
            left = a2_s[at_rows(i), :]
            grad = dy_s[at_rows(i), :]
            for n in range(2 * width // TILE):
                cols = slice(n * TILE, (n + 1) * TILE)
                s, inner = (n * TILE) // width, (n * TILE) % width
                u = dot(left, wu_s[:, cols]) + small_s[s, 0:1, inner : inner + TILE]
                g, slope = gelu_pair(u)
                gb_s[at_rows(i), cols] = g.astype(BF16)
                du = (dot_nt(grad, wd_s[cols, :]) * slope).astype(BF16)
                du_s[at_rows(i), cols] = du
                acc_s[6 + s, :, inner : inner + TILE] += fold(du.astype(F32))
            send_s[at_rows(i), :] = dot_nt(du_s[at_rows(i), :], wu_s[...]).astype(BF16)
            swap(i, rb_s, K_B).start()
            lower = dot(gb_s[at_rows(i), :], wd_s[...])
            ys_s[at_rows(i), :] = (lower + 0.5 * (r_s[at_rows(i), :] + outb[1:2, :])).astype(BF16)
            for cp in y_copies(i):
                cp.start()

        loop(CHUNKS, middle)
        end_d = grads_pair(3, dy_s, gb_s, total, (0, width), (width, 2 * width))
        end_u = grads_pair(2, a2_s, du_s, total, (0, width), (width, 2 * width))
        end_d()
        z_start(3)
        end_u()
        z_start(2)

        dq_s, drb_s = gb_s, a2_s
        for s in range(2):
            dq_s[0:total, s * QKV + 3 * WIDE : (s + 1) * QKV] = jnp.zeros((total, QKV - 3 * WIDE), BF16)

        def attend_back(i):
            swap(i, rb_s, K_B).wait()

            def back_norm(j):
                at = strip_rows(i, j)
                grad = send_s[at, :].astype(F32) + rb_s[at, :].astype(F32)
                unit, inverse = unit_of(r_s[at, :])
                dr = dy_s[at, :].astype(F32) + norm_back(grad, unit, inverse, own_gain[1])
                r_s[at, :] = dr
                drb_s[at, :] = dr.astype(BF16)
                acc_s[1] += fold(grad * unit)
                acc_s[3] += fold(grad)
                acc_s[4] += fold(dr)

            loop(strips, back_norm)
            do_s[0:rows, :] = dot_nt(drb_s[at_rows(i), :], wp_s[...]).astype(BF16)
            for h in range(HEADS):
                qc, kc, vc, oc = head_at(h)
                weights = p_s[i * HEADS + h, 0:rows, 0:span]
                grad_o = do_s[0:rows, oc]
                keys = qkv_s[key_rows(i), kc]
                slope = dot_nt(grad_o, qkv_s[key_rows(i), vc])
                ds = (weights * (slope - jnp.sum(slope * weights, axis=-1, keepdims=True))).astype(BF16)
                dq = dot(ds, keys).astype(BF16) * (HEAD**-0.5)
                dk = dot_tn(ds, qkv_s[q_rows(i), qc])
                dv = dot_tn(weights.astype(BF16), grad_o)
                dq_s[at_rows(i), qc] = dq.astype(BF16)
                if text:
                    hc = slice(h * HEAD, (h + 1) * HEAD)
                    hv = slice((HEADS + h) * HEAD, (HEADS + h + 1) * HEAD)
                    dkv_s[key_rows(i), hc] += dk
                    dkv_s[key_rows(i), hv] += dv
                else:
                    dq_s[at_rows(i), kc] = dk.astype(BF16)
                    dq_s[at_rows(i), vc] = dv.astype(BF16)

        def send_c(i):
            if text:
                for s in range(2):
                    k0 = s * QKV + WIDE
                    dq_s[at_rows(i), k0 : k0 + WIDE] = dkv_s[q_rows(i), s * WIDE : (s + 1) * WIDE].astype(BF16)
                    v0 = 2 * WIDE + s * WIDE
                    dq_s[at_rows(i), k0 + WIDE : k0 + 2 * WIDE] = dkv_s[q_rows(i), v0 : v0 + WIDE].astype(BF16)
            grad = dq_s[at_rows(i), 0 : 2 * QKV]
            send_s[at_rows(i), :] = dot_nt(grad, wq_s[...]).astype(BF16)
            swap(i, rc_s, K_C).start()
            for s in range(2):
                acc_s[8 + s, :, 0:QKV] += fold(grad[:, s * QKV : (s + 1) * QKV].astype(F32))

        if text:

            def backward(i):
                @pl.when(i < CHUNKS)
                def _():
                    attend_back(i)

                @pl.when(i > 0)
                def _():
                    send_c(i - 1)

            loop(CHUNKS + 1, backward)
        else:

            def backward(i):
                attend_back(i)
                send_c(i)

            loop(CHUNKS, backward)
        end_q = grads_pair(0, a1_s, dq_s, total, (0, QKV), (QKV, 2 * QKV))
        end_p = grads_pair(1, drb_s, o_s, total, (0, MIX), (MIX, 2 * MIX))
        end_q()
        z_start(0)
        end_p()
        z_start(1)

        def own_img(i):
            return img_out.at[pl.ds(pl.multiple_of(core * n_img + i * rows_i, 16), rows_i)]

        def own_txt(i):
            return txt_out.at[pl.ds(pl.multiple_of(core * n_txt + i * rows_t, 16), rows_t)]

        def img_copies(i):
            src = fin_s.at[pl.ds(pl.multiple_of(i * rows_i, 16), rows_i)]
            return local(src, own_img(i), 8 + i), remote(src, own_img(i), K_OI, i, sib)

        def txt_copies(i):
            src = ys_s.at[pl.ds(pl.multiple_of(i * rows_t, 16), rows_t)]
            return local(src, own_txt(i), 12 + i), remote(src, own_txt(i), K_OT, i, sib)

        def dx_copies(i):
            src = rb_s.at[pl.ds(pl.multiple_of(i * rows_t, 16), rows_t)]
            return remote(src, own_txt(i), K_T1, i, across), remote(src, own_txt(i), K_T2, i, across_sib)

        if text:

            def own_y(i):
                y_copies(i)[0].wait()
                at = at_rows(i)
                ys_s[at, :] = (ys_s[at, :].astype(F32) + yt_s[at, :].astype(F32)).astype(BF16)
                for cp in txt_copies(i):
                    cp.start()

            def image_y(i):
                at = pl.ds(pl.multiple_of(i * rows_i, 16), rows_i)
                remote(y1_s.at[at], y1_s.at[at], K_Y1, i, across).wait_recv()
                remote(y2_s.at[at], y2_s.at[at], K_Y2, i, across_peer).wait_recv()
                fin_s[at, :] = (y1_s[at, :].astype(F32) + y2_s[at, :].astype(F32)).astype(BF16)
                for cp in img_copies(i):
                    cp.start()

        def last(i):
            swap(i, rc_s, K_C).wait()

            def body(j):
                at = strip_rows(i, j)
                grad = send_s[at, :].astype(F32) + rc_s[at, :].astype(F32)
                unit, inverse = unit_of(x_s[at, :].astype(F32))
                dx = (r_s[at, :] + norm_back(grad, unit, inverse, own_gain[0])).astype(BF16)
                if text:
                    rb_s[at, :] = dx
                else:
                    fin_s[at, :] = dx
                acc_s[0] += fold(grad * unit)
                acc_s[2] += fold(grad)

            loop(strips, body)
            for cp in dx_copies(i) if text else img_copies(i):
                cp.start()

        if text:
            loop(CHUNKS, own_y)
        loop(CHUNKS, last)

        order = (0, 1, 2, 3, 4, 5, 7, 6, 9, 8, 10, 11, 12, 13, 14, 15)
        sums = jnp.sum(acc_s[...], axis=1)
        vec_s[0] = sums
        for row, src in enumerate(order):
            vec_s[1, row : row + 1, :] = sums[src : src + 1, :]
        v_sib = remote(vec_s.at[1], vrec_s, K_S, 1, sib)
        v_sib.start()
        z_finish(3)
        z_finish(2)
        v_sib.wait()
        vec_s[0] = vec_s[0] + vrec_s[...]
        if z_inside:
            vall_s[d] = vec_s[0]

            def v_copy(k):
                to = lax.rem(d + k, dp_size)
                return remote(vec_s.at[0], vall_s.at[d], K_Z + 4, k - 1, (p, to, t))

            for k in offsets:
                v_copy(k).start()
        if text:
            loop(CHUNKS, image_y)
        z_finish(0)
        z_finish(1)
        if z_inside:
            for k in offsets:
                v_copy(k).wait_send()
            for k in offsets:
                back = lax.rem(d + dp_size - k, dp_size)
                remote(vall_s.at[back], vall_s.at[back], K_Z + 4, k - 1, (p, back, t)).wait_recv()
            totals = vall_s[0]
            for k in range(1, dp_size):
                totals = totals + vall_s[k]
            vec_out[...] = totals
        else:
            vec_out[...] = vec_s[0]

        def finish(i):
            if text:
                dy_to_image(i).wait_send()
                for cp in dx_copies(i):
                    cp.wait_send()
                here, there = txt_copies(i)
                here.wait()
                there.wait()
            else:
                x_to_text(i).wait_send()
                for cp in y_copies(i):
                    cp.wait_send()
                for cp in dx_copies(i):
                    cp.wait_recv()
            here, there = img_copies(i)
            here.wait()
            there.wait()

        loop(CHUNKS, finish)
        for a in range(4):
            z_end(a)

    @pl.when(image_here)
    def _():
        one_layer(False)

    @pl.when(jnp.logical_not(image_here))
    def _():
        one_layer(True)


def per_device(
    image_side, text_side, caption_lengths, norm_gains, norm_shifts, w_qkv, bias_qv, w_proj, out_bias, w_up, bias_up, w_down,
):
    dp_size = lax.axis_size("dp")
    core = lax.rem(lax.axis_index("tensor"), 2)
    images, keys_i, width = image_side.shape[1:]
    blocks, length = text_side.shape[1:3]
    per_core = images // 2
    rows_i = -(-(per_core // CHUNKS * keys_i) // 16) * 16
    rows_t = length * (blocks // 2) // CHUNKS
    share = width // dp_size
    z_inside = 1 < dp_size <= 4 and share % 16 == 0

    img = lax.dynamic_slice_in_dim(image_side[0], core * per_core, per_core, 0)
    img = jnp.pad(img, ((0, 0), (0, rows_i - keys_i), (0, 0))).reshape(per_core * rows_i, width)
    txt = lax.dynamic_slice_in_dim(text_side[0], core, 1, 0)[0]
    bounds = jnp.cumsum(lax.dynamic_slice_in_dim(caption_lengths, core, 1, 0)[0])
    places = jnp.arange(length, dtype=jnp.int32)
    segment = jnp.sum((places[:, None] >= bounds[None, :]).astype(jnp.int32), axis=1)
    seg_col = segment[:, None]
    seg_row = jnp.pad(segment, (rows_t, rows_t), constant_values=-1)[None]
    wq = jnp.pad(w_qkv[0].reshape(width, 3 * WIDE), ((0, 0), (0, QKV - 3 * WIDE)))
    lane = jnp.zeros((WIDE,), F32)
    small = jnp.concatenate([bias_up[0], bias_qv[0, 0], lane, bias_qv[0, 1], jnp.zeros((QKV - 3 * WIDE,), F32)])
    small = jnp.broadcast_to(small[None], (8, small.shape[0]))

    n_i, n_t = rows_i * CHUNKS, rows_t * CHUNKS
    columns = (QKV, MIX, width, width)
    sds = jax.ShapeDtypeStruct
    grad_type = (lambda w: sds((share, w), F32)) if z_inside else (lambda w: sds((width, w), BF16))
    outs = [sds((2 * n_i, width), BF16), sds((2 * n_t, width), BF16)]
    outs += [grad_type(w) for w in columns] + [sds((16, width), F32)]
    any_spec, vmem_spec = pl.BlockSpec(memory_space=pl.ANY), pl.BlockSpec(memory_space=pltpu.VMEM)
    v = pltpu.VMEM
    scratch = [
        v((n_i, width), BF16), v((n_i, width), BF16),
        v((width, 2 * QKV), BF16), v((2 * MIX, width), BF16), v((width, 2 * width), BF16), v((2 * width, width), BF16),
        v((2, 8, width + QKV), F32),
        v((n_i, width), BF16), v((max(n_i, n_t + 2 * rows_t), 2 * QKV), BF16), v((n_i, 2 * MIX), BF16), v((n_i, width), F32),
        v((n_i, width), BF16), v((n_i, 2 * width), BF16), v((n_i, 2 * width), BF16),
        v((CHUNKS * HEADS, max(rows_i, rows_t), max(-(-rows_i // 128) * 128, 3 * rows_t)), F32),
        v((n_t + 2 * rows_t, 2 * HEADS * HEAD), F32), v((max(rows_i, rows_t), 2 * MIX), BF16),
        v((n_i, width), BF16), v((n_i, width), BF16), v((n_i, width), BF16), v((n_i, width), BF16),
        v((n_i, width), BF16), v((n_t, width), BF16), v((n_i, width), BF16), v((n_i, width), BF16), v((n_i, width), BF16),
        v((16, 8, width), F32), v((2, 16, width), F32), v((16, width), F32), v((dp_size if z_inside else 1, 16, width), F32),
    ]
    scratch += [v((width, w), BF16) for w in columns] + [v((width, w), BF16) for w in columns]
    if z_inside:
        scratch += [v((dp_size - 1, share, w), BF16) for w in columns] + [v((share, w), F32) for w in columns]
    dma = pltpu.SemaphoreType.DMA
    scratch += [dma((4 * N_KINDS,)), dma((4 * N_KINDS,)), dma((24,))]
    img_out, txt_out, g_q, g_p, g_u, g_d, vec = pl.pallas_call(
        partial(layers_kernel, rows_i, rows_t, keys_i, dp_size, z_inside),
        out_shape=outs,
        in_specs=[any_spec] * 7 + [vmem_spec] * 5,
        out_specs=[any_spec] * 6 + [vmem_spec],
        scratch_shapes=scratch,
        compiler_params=pltpu.CompilerParams(collective_id=0, has_side_effects=True, vmem_limit_bytes=60 << 20),
    )(
        img, txt, wq, w_proj[0], w_up[0], w_down[0], small, norm_gains[0], norm_shifts[0], out_bias[0], seg_col, seg_row,
    )
    if not z_inside:
        def scatter(grad):
            return lax.psum_scatter(grad, "dp", scatter_dimension=0, tiled=True).astype(F32)

        g_q, g_p, g_u, g_d = (scatter(g) for g in (g_q[:, : 3 * WIDE], g_p[:, :WIDE], g_u, g_d))
        vec = lax.psum(vec, "dp")
    image_result = img_out.reshape(images, rows_i, width)[:, :keys_i][None]
    text_result = txt_out.reshape(blocks, length, width)[None]
    return (
        image_result,
        text_result,
        vec[0:2][None],
        vec[2:4][None],
        g_q[:, : 3 * WIDE].reshape(share, 3, WIDE)[None],
        jnp.stack([vec[8, 0:WIDE], vec[8, 2 * WIDE : 3 * WIDE]])[None],
        g_p[:, :WIDE].T[None],
        vec[4:6][None],
        g_u[None],
        vec[6][None],
        g_d.T[None],
    )


def solution(mesh):
    placed = (
        P("pipe", "dp", None, None),
        P("pipe", "dp", None, None),
        P("dp", None),
        P("pipe", None, None),
        P("pipe", None, None),
        P("pipe", None, None, "tensor"),
        P("pipe", None, "tensor"),
        P("pipe", "tensor", None),
        P("pipe", None, None),
        P("pipe", None, "tensor"),
        P("pipe", "tensor"),
        P("pipe", "tensor", None),
    )
    return jax.shard_map(
        per_device,
        mesh=mesh,
        in_specs=placed,
        out_specs=(
            P("pipe", "dp", None, None),
            P("pipe", "dp", None, None),
            P("pipe", None, None),
            P("pipe", None, None),
            P("pipe", "dp", None, "tensor"),
            P("pipe", None, "tensor"),
            P("pipe", "tensor", "dp"),
            P("pipe", None, None),
            P("pipe", "dp", "tensor"),
            P("pipe", "tensor"),
            P("pipe", "tensor", "dp"),
        ),
        check_vma=False,
    )
```

time: 832 us -> 185 us (0.22)
  waiting for transfers between devices: 414 us -> 0 us
  Pallas kernels: 0 us -> 158 us
  matrix products: 150 us -> 0 us
  local copies, waits for them, and re-layouts: 131 us -> 24 us
  other arithmetic: 73.4 us -> 1.55 us
  blocking collectives: 19.6 us -> 0 us
  starting transfers between devices: 18.9 us -> 0 us
  between operations: 17.2 us -> 0.76 us
    psum x3 -> x0, waiting for transfers between devices: 399 us -> none  [the longest x1 148 us: layer_backward(): lax.psum(lower_part.astype(jnp.bfloat16), 'tensor').astype(jnp.float32)]
    pallas_call x0 -> x1, Pallas kernels: none -> 158 us  [per_device(): pl.pallas_call(partial(layers_kernel, rows_i, rows_t, keys_i, dp_size, z_...]
    dot_general x68 -> x0, matrix products: 143 us -> none  [the longest x4 25.8 us: layer_forward(): jnp.dot(normed_two_low, w_up, preferred_element_type=jnp.float32) + bias_up]
    reduce_sum x31 -> x1, other arithmetic: 43.1 us -> 0.09 us  [per_device(): jnp.sum((places[:, None] >= bounds[None, :]).astype(jnp.int32), axis=1)]
    unnamed x496 -> x17, local copies, waits for them, and re-layouts: 37.1 us -> 8.27 us
    another operation x30 -> x2, local copies, waits for them, and re-layouts: 26.4 us -> 2.37 us  [the longest x1 1.53 us: per_device(): w_qkv[0].reshape(width, 3 * WIDE)]
    convert_element_type x14 -> x0, local copies, waits for them, and re-layouts: 20.6 us -> none  [the longest x4 7.58 us: layer_forward(): normed.astype(jnp.bfloat16)]
    psum x1 -> x0, blocking collectives: 19.6 us -> none  [per_device(): lax.psum((grad_sums[0], grad_sums[1], grad_sums[3], grad_sums[5], grad_su...]
  transfers between devices with their start and end apart: 15 -> 0, of which waited for: 5 -> 0; matrix products, arithmetic and copies ran while one was open for 34% -> 0% of each run, Pallas kernels for 0% -> 0%
where the time goes in v1:
time: 185 us; the launch traced here: 184 us
  Pallas kernels  158 us (85%)
  local copies, waits for them, and re-layouts  24 us (13%)
    pallas_call x1, Pallas kernels, per_device(): pl.pallas_call(partial(layers_kernel, rows_i, rows_t, keys_i, dp_size, z_...  158 us
    unnamed x17, local copies, waits for them, and re-layouts  8.27 us

profile of v1, /device:TPU:0, one launch (start us, length us, event | category | flops | bytes accessed | tf_op | source)
XLA Modules:
  0.0 184.2 jit_solution(12806007397537731987)
XLA Ops:
  0.6 0.0 copy-start
  0.7 0.8 fusion
  1.5 0.2 reduce-window.8
  1.7 0.1 convert_reduce_fusion
  1.8 0.8 fusion.2
  2.6 0.6 broadcast_in_dim.48.seg_row
  3.1 0.7 reduce
  3.9 0.1 concatenate.3
  3.9 0.6 broadcast_in_dim.46.small
  4.6 0.9 copy.36.seg_col
  5.4 2.1 %dynamic-slice_bitcast_fusion.txt_own = bf16[512,768]{1,0:T(8,128)(2,1)} fusion(bf16[1,2,512,768]{3,2,1,0:T(8,128)(2,1)} %param.13, s32[]{:T(128)S(6)} %select_n.8), kind=kLoop, calls=%fused_computation.2 | loop fusion | bytes 1572868 | tf_op jit(solution)/shard_map/squeeze | solution.py:639
  7.5 1.5 copy.35
  9.0 1.0 pad.13.w_qkv
  10.1 0.6 constant_dynamic-slice_fusion.1
  10.7 0.1 copy.46
  10.8 1.1 pad.12
  12.0 157.9 %shard_map.203 = (bf16[1664,768]{1,0:T(8,128)(2,1)}, bf16[1024,768]{1,0:T(8,128)(2,1)}, f32[192,640]{1,0:T(8,128)}, f32[192,256]{1,0:T(8,128)}, f32[192,768]{1,0...) custom-call(bf16[832,768]{1,0:T(8,128)(2,1)} %bitcast.42, bf16[512,768]{1,0:T(8,128)(2,1)} %dynamic-slice_bitcast_fusion.txt_own, ...), custom_call_target="tpu_custom_call" | custom-call | tf_op jit(solution)/shard_map/pallas_call | solution.py:675
  169.8 1.9 %slice.44 = bf16[8,197,768]{2,1,0:T(8,128)(2,1)S(1)} slice(bf16[8,208,768]{2,1,0:T(8,128)(2,1)} %bitcast.45), slice={[0:8], [0:197], [0:768]} | slice | bytes 4841472 | tf_op jit(solution)/shard_map/slice | solution.py:691
  171.7 0.0 copy-start.4
  171.7 0.0 copy-start.3
  171.7 1.9 %copy.45 = bf16[8,197,768]{2,0,1:T(8,128)(2,1)} copy(bf16[8,197,768]{2,1,0:T(8,128)(2,1)S(1)} %slice.44) | data formatting | bytes 4841472
  173.6 0.7 fusion.1
  174.3 0.6 maximum_bitcast_fusion
  174.9 1.3 slice.43
  176.2 1.5 slice_bitcast_fusion.1
  177.7 0.0 copy-done.4
  177.7 0.8 copy.40
  178.5 0.2 copy.38
  178.7 1.1 copy.39
  179.8 2.7 %copy.50 = bf16[1,2,512,768]{3,2,1,0:T(8,128)(2,1)} copy(bf16[1,2,512,768]{3,2,1,0:T(8,128)(2,1)} %bitcast.47) | data formatting | bytes 3145728
  182.5 0.8 copy.51
  183.4 0.8 copy.52
  (10 shorter events, 0.0 us)
Async XLA Ops:
  0.6 9.4 %copy-start = (bf16[1,8,197,768]{3,1,2,0:T(8,128)(2,1)S(1)}, bf16[1,8,197,768]{3,1,2,0:T(8,128)(2,1)}, u32[]{:S(2)}) copy-start(bf16[1,8,197,768]{3,1,2,0:T(8,128)(2,1)} %param.12) | copy-start | bytes 7262212
  171.7 6.0 %copy-start.4 = (f32[192,256]{1,0:T(8,128)S(1)}, f32[192,256]{1,0:T(8,128)}, u32[]{:S(2)}) copy-start(f32[192,256]{1,0:T(8,128)} %get-tuple-element.22) | copy-start | bytes 589828
  171.7 6.8 %copy-start.3 = (f32[192,640]{1,0:T(8,128)S(1)}, f32[192,640]{1,0:T(8,128)}, u32[]{:S(2)}) copy-start(f32[192,640]{1,0:T(8,128)} %get-tuple-element.21) | copy-start | bytes 1474564
  179.8 2.8 %copy-start.2 = (f32[192,768]{1,0:T(8,128)S(1)}, f32[192,768]{1,0:T(8,128)}, u32[]{:S(2)}) copy-start(f32[192,768]{1,0:T(8,128)} %get-tuple-element.23) | copy-start | bytes 1769476
  179.8 3.6 %copy-start.1 = (f32[192,768]{1,0:T(8,128)S(1)}, f32[192,768]{1,0:T(8,128)}, u32[]{:S(2)}) copy-start(f32[192,768]{1,0:T(8,128)} %get-tuple-element.24) | copy-start | bytes 1769476

commit v2 on v1

--- a/solution.py
+++ b/solution.py
@@ -18,12 +18,14 @@
 MASKED = -1000000000.0
 CHUNKS = 4
 STRIP = 16
+BLOCK = 208
 QKV = 640
 MIX = 256
+PAD = MIX - WIDE
 TILE = 256
 
-K_IN, K_A, K_B, K_C, K_Y1, K_Y2, K_YT, K_OI, K_OT, K_T1, K_T2, K_W, K_S, K_G, K_Z = range(15)
-N_KINDS = K_Z + 5
+K_IN, K_A, K_B, K_C, K_Y1, K_Y2, K_YT, K_OI, K_OT, K_T1, K_W, K_S, K_G, K_V, K_Z = range(15)
+N_KINDS = K_Z + 3
 
 
 def dot(a, b):
@@ -72,13 +74,13 @@
 def layers_kernel(
     rows_i, rows_t, keys_i, dp_size, z_inside,
     img_own, txt_own, w_qkv, w_proj, w_up, w_down, small, gains, shifts, outb, seg_col, seg_row,
-    img_out, txt_out, g_qkv, g_proj, g_up, g_down, vec_out,
+    img_out, txt_out, g_mix, g_up, g_down, vec_out,
     x_s, dy_s, wq_s, wp_s, wu_s, wd_s, small_s, a1_s, qkv_s, o_s, r_s, a2_s, gb_s, du_s, p_s, dkv_s, do_s,
     send_s, ra_s, rb_s, rc_s, ys_s, yt_s, y1_s, y2_s, fin_s, acc_s, vec_s, vrec_s, vall_s,
-    gs_q, gs_p, gs_u, gs_d, gr_q, gr_p, gr_u, gr_d, *rest,
+    gs_x, gs_u, gs_d, gr_x, gr_u, gr_d, *rest,
 ):
     if z_inside:
-        zr_q, zr_p, zr_u, zr_d, zf_q, zf_p, zf_u, zf_d, ssem, rsem, lsem = rest
+        z1_s, z2_s, zf_s, ssem, rsem, lsem = rest
     else:
         ssem, rsem, lsem = rest
     width = x_s.shape[1]
@@ -88,9 +90,9 @@
     peer_t = lax.rem(t + 2, 4)
     other = 1 - p
     sib, peer = (p, d, sib_t), (p, d, peer_t)
-    across, across_peer, across_sib = (other, d, t), (other, d, peer_t), (other, d, sib_t)
+    across = (other, d, t)
     offsets = range(1, dp_size) if z_inside else range(0)
-    partners = [sib, peer, across, across_peer, across_sib]
+    partners = [sib, peer, across]
     partners += [(p, lax.rem(d + k, dp_size), t) for k in offsets]
 
     def remote(src, dst, kind, slot, to):
@@ -108,7 +110,7 @@
     n_txt = rows_t * CHUNKS
 
     wq_own = local(w_qkv, wq_s.at[:, 0:QKV], 0)
-    wp_own = local(w_proj, wp_s.at[0:WIDE], 1)
+    wp_own = local(w_proj, wp_s.at[PAD:MIX], 1)
     wu_own = local(w_up, wu_s.at[:, 0:width], 2)
     wd_own = local(w_down, wd_s.at[0:width], 3)
     sm_own = local(small, small_s.at[0], 4)
@@ -128,9 +130,9 @@
     wp_own.start()
     wu_own.start()
     wd_own.start()
-    zero_rows = jnp.zeros((MIX - WIDE, width), BF16)
-    wp_s[WIDE:MIX, :] = zero_rows
-    wp_s[MIX + WIDE :, :] = zero_rows
+    zero_rows = jnp.zeros((PAD, width), BF16)
+    wp_s[0:PAD, :] = zero_rows
+    wp_s[MIX : MIX + PAD, :] = zero_rows
     acc_s[...] = jnp.zeros_like(acc_s)
 
     barrier = pltpu.get_barrier_semaphore()
@@ -140,7 +142,7 @@
 
     sm_sib = remote(small, small_s.at[1], K_S, 0, sib)
     wq_sib = remote(w_qkv, wq_s.at[:, QKV:], K_W, 0, sib)
-    wp_sib = remote(w_proj, wp_s.at[MIX : MIX + WIDE], K_W, 1, sib)
+    wp_sib = remote(w_proj, wp_s.at[MIX + PAD :], K_W, 1, sib)
     wu_sib = remote(w_up, wu_s.at[:, width:], K_W, 2, sib)
     wd_sib = remote(w_down, wd_s.at[width:], K_W, 3, sib)
 
@@ -170,27 +172,18 @@
     own_gain = [gains[0:1, :], gains[1:2, :]]
     own_shift = [shifts[0:1, :], shifts[1:2, :]]
 
-    g_arrays = [(gs_q, gr_q), (gs_p, gr_p), (gs_u, gr_u), (gs_d, gr_d)]
+    g_arrays = [(gs_x, gr_x, g_mix), (gs_u, gr_u, g_up), (gs_d, gr_d, g_down)]
 
     def g_exchange(a):
         return remote(g_arrays[a][0], g_arrays[a][1], K_G, a, sib)
 
-    def grads_pair(a, left, right, n, own_cols, sib_cols):
-        mine, theirs = g_arrays[a]
+    def grads_pair(a, product):
+        mine, theirs = g_arrays[a][0:2]
         tiles = width // TILE
 
-        def part(cols):
-            def body(m):
-                at = pl.ds(pl.multiple_of(m * TILE, TILE), TILE)
-                return at, dot_tn(left[0:n, at], right[0:n, cols[0] : cols[1]])
-
-            return body
-
-        first, second = part(sib_cols), part(own_cols)
-
         def send_half(m):
-            at, value = first(m)
-            mine[at, :] = value.astype(BF16)
+            at = pl.ds(pl.multiple_of(m * TILE, TILE), TILE)
+            mine[at, :] = product(at, 1).astype(BF16)
 
         loop(tiles, send_half)
         g_exchange(a).start()
@@ -199,58 +192,62 @@
             g_exchange(a).wait()
 
             def own_half(m):
-                at, value = second(m)
-                mine[at, :] = (value + theirs[at, :].astype(F32)).astype(BF16)
+                at = pl.ds(pl.multiple_of(m * TILE, TILE), TILE)
+                mine[at, :] = (product(at, 0) + theirs[at, :].astype(F32)).astype(BF16)
 
             loop(tiles, own_half)
 
         return finish
 
-    z_sets = [(gs_q, zr_q, zf_q, g_qkv), (gs_p, zr_p, zf_p, g_proj), (gs_u, zr_u, zf_u, g_up), (gs_d, zr_d, zf_d, g_down)] if z_inside else []
     share = width // dp_size
-
-    def z_copy(a, k):
-        whole, landing = z_sets[a][0:2]
-        to = lax.rem(d + k, dp_size)
-        rows = pl.ds(pl.multiple_of(to * share, 16), share)
-        return remote(whole.at[rows], landing.at[k - 1], K_Z + a, k - 1, (p, to, t))
-
-    out_plain = [(gs_q, g_qkv), (gs_p, g_proj), (gs_u, g_up), (gs_d, g_down)]
+    parity = lax.rem(d, 2)
+    upper = d // 2
+    near = d + 1 - 2 * parity
+    far = d + 2 - 4 * upper if z_inside else d
+
+    def share_rows(at):
+        return pl.ds(pl.multiple_of(at * share, 16), share)
+
+    def z_near(a, k):
+        src = g_arrays[a][0].at[share_rows(1 - parity + 2 * k)]
+        return remote(src, z1_s.at[a, k], K_Z, 3 * k + a, (p, near, t))
+
+    def z_far(a):
+        return remote(g_arrays[a][0].at[share_rows(far)], z2_s.at[a], K_Z, 6 + a, (p, far, t))
 
     def z_start(a):
         if z_inside:
-            for k in offsets:
-                z_copy(a, k).start()
+            for k in range(2):
+                z_near(a, k).start()
         else:
-            local(out_plain[a][0], out_plain[a][1], 20 + a).start()
+            local(g_arrays[a][0], g_arrays[a][2], 20 + a).start()
+
+    def z_middle(a):
+        if z_inside:
+            for k in range(2):
+                z_near(a, k).wait()
+            mine = g_arrays[a][0]
+            rows = share_rows(far)
+            mine[rows, :] = (mine[rows, :].astype(F32) + z1_s[a, 1 - upper].astype(F32)).astype(BF16)
+            z_far(a).start()
 
     def z_finish(a):
         if z_inside:
-            whole, landing, final, result = z_sets[a]
-            for k in offsets:
-                z_copy(a, k).wait()
-
-            def body(j):
-                at = pl.ds(pl.multiple_of(j * STRIP, STRIP), STRIP)
-                rows = pl.ds(pl.multiple_of(d * share + j * STRIP, STRIP), STRIP)
-                total = whole[rows, :].astype(F32)
-                for k in offsets:
-                    total = total + landing[k - 1, at, :].astype(F32)
-                final[at, :] = total
-
-            loop(share // STRIP, body)
-            local(final, result, 20 + a).start()
+            z_far(a).wait()
+            total = g_arrays[a][0][share_rows(d), :].astype(F32) + z1_s[a, upper].astype(F32)
+            zf_s[a] = total + z2_s[a].astype(F32)
+            local(zf_s.at[a], g_arrays[a][2], 20 + a).start()
 
     def z_end(a):
         if z_inside:
-            local(z_sets[a][2], z_sets[a][3], 20 + a).wait()
+            local(zf_s.at[a], g_arrays[a][2], 20 + a).wait()
         else:
-            local(out_plain[a][0], out_plain[a][1], 20 + a).wait()
+            local(g_arrays[a][0], g_arrays[a][2], 20 + a).wait()
 
     def one_layer(text):
         rows = rows_t if text else rows_i
         total = rows * CHUNKS
-        strips = rows // STRIP
+        cuts = [(o, min(BLOCK, rows - o)) for o in range(0, rows, BLOCK)]
         q_off = rows_t if text else 0
 
         def at_rows(i):
@@ -259,8 +256,9 @@
         def q_rows(i):
             return pl.ds(pl.multiple_of(i * rows + q_off, 16), rows)
 
-        def strip_rows(i, j):
-            return pl.ds(pl.multiple_of(i * rows + j * STRIP, STRIP), STRIP)
+        def by_strips(i, body):
+            for o, size in cuts:
+                body(pl.ds(pl.multiple_of(i * rows + o, STRIP), size))
 
         def swap(i, landing, kind):
             return remote(send_s.at[at_rows(i)], landing.at[at_rows(i)], kind, i, peer)
@@ -285,18 +283,17 @@
         else:
             img_in.wait()
         for s in range(2):
-            o_s[0:total, s * MIX + WIDE : (s + 1) * MIX] = jnp.zeros((total, MIX - WIDE), BF16)
+            o_s[0:total, s * MIX : s * MIX + PAD] = jnp.zeros((total, PAD), BF16)
 
         def project(i):
             if text:
                 wait_input(i)
 
-            def first_norm(j):
-                at = strip_rows(i, j)
+            def first_norm(at):
                 unit, _ = unit_of(x_s[at, :].astype(F32))
                 a1_s[at, :] = (unit * own_gain[0] + own_shift[0]).astype(BF16)
 
-            loop(strips, first_norm)
+            by_strips(i, first_norm)
             left = a1_s[at_rows(i), :]
             lanes = lax.broadcasted_iota(jnp.int32, (1, QKV), 1)
             factor = jnp.where(lanes < WIDE, HEAD**-0.5, 1.0).astype(F32)
@@ -308,7 +305,7 @@
         def head_at(h):
             s, hh = h // HALF, h % HALF
             base = s * QKV + hh * HEAD
-            return slice(base, base + HEAD), slice(base + WIDE, base + WIDE + HEAD), slice(base + 2 * WIDE, base + 2 * WIDE + HEAD), slice(s * MIX + hh * HEAD, s * MIX + hh * HEAD + HEAD)
+            return slice(base, base + HEAD), slice(base + WIDE, base + WIDE + HEAD), slice(base + 2 * WIDE, base + 2 * WIDE + HEAD), slice(s * MIX + PAD + hh * HEAD, s * MIX + PAD + hh * HEAD + HEAD)
 
         span = 3 * rows_t if text else rows_i
 
@@ -339,15 +336,23 @@
             swap(i, ra_s, K_A).start()
 
         if text:
-            loop(CHUNKS, project)
-            wp_own.wait()
-            wp_sib.wait()
 
             def forward(i):
-                attend(i)
-                send_a(i)
-
-            loop(CHUNKS, forward)
+                @pl.when(i < CHUNKS)
+                def _():
+                    project(i)
+
+                @pl.when(i == 1)
+                def _():
+                    wp_own.wait()
+                    wp_sib.wait()
+
+                @pl.when(i > 0)
+                def _():
+                    attend(i - 1)
+                    send_a(i - 1)
+
+            loop(CHUNKS + 1, forward)
         else:
 
             def forward(i):
@@ -371,25 +376,30 @@
             at = at_rows(i)
             if text:
                 return [remote(ys_s.at[at], yt_s.at[at], K_YT, i, peer)]
-            return [
-                remote(ys_s.at[at], y1_s.at[at], K_Y1, i, across),
-                remote(ys_s.at[at], y2_s.at[at], K_Y2, i, across_peer),
-            ]
+            return [remote(ys_s.at[at], y1_s.at[at], K_Y1, i, across)]
+
+        def y_relay(i):
+            at = pl.ds(pl.multiple_of(i * rows_i, 16), rows_i)
+            return remote(y1_s.at[at], y2_s.at[at], K_Y2, i, peer)
+
+        def hand_on(i):
+            at = pl.ds(pl.multiple_of(i * rows_i, 16), rows_i)
+            remote(y1_s.at[at], y1_s.at[at], K_Y1, i, across).wait_recv()
+            y_relay(i).start()
 
         def middle(i):
             if not text:
                 wait_input(i)
             swap(i, ra_s, K_A).wait()
 
-            def second_norm(j):
-                at = strip_rows(i, j)
+            def second_norm(at):
                 r = x_s[at, :].astype(F32) + (send_s[at, :].astype(F32) + ra_s[at, :].astype(F32)) + outb[0:1, :]
                 r_s[at, :] = r
                 unit, _ = unit_of(r)
                 a2_s[at, :] = (unit * own_gain[1] + own_shift[1]).astype(BF16)
                 acc_s[5] += fold(dy_s[at, :].astype(F32))
 
-            loop(strips, second_norm)
+            by_strips(i, second_norm)
             left = a2_s[at_rows(i), :]
             grad = dy_s[at_rows(i), :]
             for n in range(2 * width // TILE):
@@ -405,16 +415,17 @@
             swap(i, rb_s, K_B).start()
             lower = dot(gb_s[at_rows(i), :], wd_s[...])
             ys_s[at_rows(i), :] = (lower + 0.5 * (r_s[at_rows(i), :] + outb[1:2, :])).astype(BF16)
-            for cp in y_copies(i):
-                cp.start()
+            if not text:
+                for cp in y_copies(i):
+                    cp.start()
 
         loop(CHUNKS, middle)
-        end_d = grads_pair(3, dy_s, gb_s, total, (0, width), (width, 2 * width))
-        end_u = grads_pair(2, a2_s, du_s, total, (0, width), (width, 2 * width))
+        end_d = grads_pair(2, lambda at, s: dot_tn(dy_s[0:total, at], gb_s[0:total, s * width : (s + 1) * width]))
+        end_u = grads_pair(1, lambda at, s: dot_tn(a2_s[0:total, at], du_s[0:total, s * width : (s + 1) * width]))
         end_d()
-        z_start(3)
+        z_start(2)
         end_u()
-        z_start(2)
+        z_start(1)
 
         dq_s, drb_s = gb_s, a2_s
         for s in range(2):
@@ -423,8 +434,7 @@
         def attend_back(i):
             swap(i, rb_s, K_B).wait()
 
-            def back_norm(j):
-                at = strip_rows(i, j)
+            def back_norm(at):
                 grad = send_s[at, :].astype(F32) + rb_s[at, :].astype(F32)
                 unit, inverse = unit_of(r_s[at, :])
                 dr = dy_s[at, :].astype(F32) + norm_back(grad, unit, inverse, own_gain[1])
@@ -434,7 +444,7 @@
                 acc_s[3] += fold(grad)
                 acc_s[4] += fold(dr)
 
-            loop(strips, back_norm)
+            by_strips(i, back_norm)
             do_s[0:rows, :] = dot_nt(drb_s[at_rows(i), :], wp_s[...]).astype(BF16)
             for h in range(HEADS):
                 qc, kc, vc, oc = head_at(h)
@@ -469,32 +479,6 @@
             for s in range(2):
                 acc_s[8 + s, :, 0:QKV] += fold(grad[:, s * QKV : (s + 1) * QKV].astype(F32))
 
-        if text:
-
-            def backward(i):
-                @pl.when(i < CHUNKS)
-                def _():
-                    attend_back(i)
-
-                @pl.when(i > 0)
-                def _():
-                    send_c(i - 1)
-
-            loop(CHUNKS + 1, backward)
-        else:
-
-            def backward(i):
-                attend_back(i)
-                send_c(i)
-
-            loop(CHUNKS, backward)
-        end_q = grads_pair(0, a1_s, dq_s, total, (0, QKV), (QKV, 2 * QKV))
-        end_p = grads_pair(1, drb_s, o_s, total, (0, MIX), (MIX, 2 * MIX))
-        end_q()
-        z_start(0)
-        end_p()
-        z_start(1)
-
         def own_img(i):
             return img_out.at[pl.ds(pl.multiple_of(core * n_img + i * rows_i, 16), rows_i)]
 
@@ -511,7 +495,10 @@
 
         def dx_copies(i):
             src = rb_s.at[pl.ds(pl.multiple_of(i * rows_t, 16), rows_t)]
-            return remote(src, own_txt(i), K_T1, i, across), remote(src, own_txt(i), K_T2, i, across_sib)
+            return remote(src, own_txt(i), K_T1, i, across)
+
+        def dx_relay(i):
+            return remote(own_txt(i), own_txt(i), K_OT, i, sib)
 
         if text:
 
@@ -524,8 +511,7 @@
 
             def image_y(i):
                 at = pl.ds(pl.multiple_of(i * rows_i, 16), rows_i)
-                remote(y1_s.at[at], y1_s.at[at], K_Y1, i, across).wait_recv()
-                remote(y2_s.at[at], y2_s.at[at], K_Y2, i, across_peer).wait_recv()
+                y_relay(i).wait()
                 fin_s[at, :] = (y1_s[at, :].astype(F32) + y2_s[at, :].astype(F32)).astype(BF16)
                 for cp in img_copies(i):
                     cp.start()
@@ -533,8 +519,7 @@
         def last(i):
             swap(i, rc_s, K_C).wait()
 
-            def body(j):
-                at = strip_rows(i, j)
+            def body(at):
                 grad = send_s[at, :].astype(F32) + rc_s[at, :].astype(F32)
                 unit, inverse = unit_of(x_s[at, :].astype(F32))
                 dx = (r_s[at, :] + norm_back(grad, unit, inverse, own_gain[0])).astype(BF16)
@@ -545,13 +530,71 @@
                 acc_s[0] += fold(grad * unit)
                 acc_s[2] += fold(grad)
 
-            loop(strips, body)
-            for cp in dx_copies(i) if text else img_copies(i):
+            by_strips(i, body)
+
+            for cp in [dx_copies(i)] if text else img_copies(i):
                 cp.start()
 
         if text:
+            hand_on(0)
+            hand_on(1)
+        if text:
+
+            def backward(i):
+                @pl.when(i < CHUNKS)
+                def _():
+                    attend_back(i)
+
+                @pl.when(i == CHUNKS - 1)
+                def _():
+                    z_middle(2)
+
+                @pl.when(i > 0)
+                def _():
+                    send_c(i - 1)
+
+                @pl.when(i > 2)
+                def _():
+                    last(i - 3)
+
+            loop(CHUNKS + 1, backward)
+        else:
+
+            def backward(i):
+                @pl.when(i == CHUNKS - 1)
+                def _():
+                    z_middle(2)
+
+                attend_back(i)
+                send_c(i)
+
+            loop(CHUNKS, backward)
+
+        def mixed_grads(at, s):
+            first = dot_tn(a1_s[0:total, at], dq_s[0:total, s * QKV : (s + 1) * QKV])
+            second = dot_tn(drb_s[0:total, at], o_s[0:total, s * MIX : (s + 1) * MIX])
+            seam = first[:, MIX * 2 :] + second[:, 0 : QKV - 2 * MIX]
+            return jnp.concatenate([first[:, : MIX * 2], seam, second[:, QKV - 2 * MIX :]], axis=1)
+
+        if text:
+            loop(CHUNKS, lambda i: y_copies(i)[0].start())
+        end_x = grads_pair(0, mixed_grads)
+        end_x()
+        z_start(0)
+        if text:
+            last(CHUNKS - 2)
+            last(CHUNKS - 1)
+            hand_on(2)
+            hand_on(3)
+            z_middle(1)
             loop(CHUNKS, own_y)
-        loop(CHUNKS, last)
+            z_middle(0)
+        else:
+            z_middle(1)
+            loop(CHUNKS - 1, last)
+            z_middle(0)
+            last(CHUNKS - 1)
+
 
         order = (0, 1, 2, 3, 4, 5, 7, 6, 9, 8, 10, 11, 12, 13, 14, 15)
         sums = jnp.sum(acc_s[...], axis=1)
@@ -560,8 +603,8 @@
             vec_s[1, row : row + 1, :] = sums[src : src + 1, :]
         v_sib = remote(vec_s.at[1], vrec_s, K_S, 1, sib)
         v_sib.start()
-        z_finish(3)
         z_finish(2)
+        z_finish(1)
         v_sib.wait()
         vec_s[0] = vec_s[0] + vrec_s[...]
         if z_inside:
@@ -569,20 +612,19 @@
 
             def v_copy(k):
                 to = lax.rem(d + k, dp_size)
-                return remote(vec_s.at[0], vall_s.at[d], K_Z + 4, k - 1, (p, to, t))
+                return remote(vec_s.at[0], vall_s.at[d], K_V, k - 1, (p, to, t))
 
             for k in offsets:
                 v_copy(k).start()
         if text:
             loop(CHUNKS, image_y)
         z_finish(0)
-        z_finish(1)
         if z_inside:
             for k in offsets:
                 v_copy(k).wait_send()
             for k in offsets:
                 back = lax.rem(d + dp_size - k, dp_size)
-                remote(vall_s.at[back], vall_s.at[back], K_Z + 4, k - 1, (p, back, t)).wait_recv()
+                remote(vall_s.at[back], vall_s.at[back], K_V, k - 1, (p, back, t)).wait_recv()
             totals = vall_s[0]
             for k in range(1, dp_size):
                 totals = totals + vall_s[k]
@@ -593,8 +635,7 @@
         def finish(i):
             if text:
                 dy_to_image(i).wait_send()
-                for cp in dx_copies(i):
-                    cp.wait_send()
+                dx_copies(i).wait_send()
                 here, there = txt_copies(i)
                 here.wait()
                 there.wait()
@@ -602,14 +643,16 @@
                 x_to_text(i).wait_send()
                 for cp in y_copies(i):
                     cp.wait_send()
-                for cp in dx_copies(i):
-                    cp.wait_recv()
+                dx_copies(i).wait_recv()
+                dx_relay(i).start()
             here, there = img_copies(i)
             here.wait()
             there.wait()
 
         loop(CHUNKS, finish)
-        for a in range(4):
+        if not text:
+            loop(CHUNKS, lambda i: dx_relay(i).wait())
+        for a in range(3):
             z_end(a)
 
     @pl.when(image_here)
@@ -632,7 +675,7 @@
     rows_i = -(-(per_core // CHUNKS * keys_i) // 16) * 16
     rows_t = length * (blocks // 2) // CHUNKS
     share = width // dp_size
-    z_inside = 1 < dp_size <= 4 and share % 16 == 0
+    z_inside = dp_size == 4 and share % 16 == 0
 
     img = lax.dynamic_slice_in_dim(image_side[0], core * per_core, per_core, 0)
     img = jnp.pad(img, ((0, 0), (0, rows_i - keys_i), (0, 0))).reshape(per_core * rows_i, width)
@@ -648,7 +691,7 @@
     small = jnp.broadcast_to(small[None], (8, small.shape[0]))
 
     n_i, n_t = rows_i * CHUNKS, rows_t * CHUNKS
-    columns = (QKV, MIX, width, width)
+    columns = (width, width, width)
     sds = jax.ShapeDtypeStruct
     grad_type = (lambda w: sds((share, w), F32)) if z_inside else (lambda w: sds((width, w), BF16))
     outs = [sds((2 * n_i, width), BF16), sds((2 * n_t, width), BF16)]
@@ -669,14 +712,14 @@
     ]
     scratch += [v((width, w), BF16) for w in columns] + [v((width, w), BF16) for w in columns]
     if z_inside:
-        scratch += [v((dp_size - 1, share, w), BF16) for w in columns] + [v((share, w), F32) for w in columns]
+        scratch += [v((3, 2, share, width), BF16), v((3, share, width), BF16), v((3, share, width), F32)]
     dma = pltpu.SemaphoreType.DMA
     scratch += [dma((4 * N_KINDS,)), dma((4 * N_KINDS,)), dma((24,))]
-    img_out, txt_out, g_q, g_p, g_u, g_d, vec = pl.pallas_call(
+    img_out, txt_out, g_x, g_u, g_d, vec = pl.pallas_call(
         partial(layers_kernel, rows_i, rows_t, keys_i, dp_size, z_inside),
         out_shape=outs,
         in_specs=[any_spec] * 7 + [vmem_spec] * 5,
-        out_specs=[any_spec] * 6 + [vmem_spec],
+        out_specs=[any_spec] * 5 + [vmem_spec],
         scratch_shapes=scratch,
         compiler_params=pltpu.CompilerParams(collective_id=0, has_side_effects=True, vmem_limit_bytes=60 << 20),
     )(
@@ -686,7 +729,7 @@
         def scatter(grad):
             return lax.psum_scatter(grad, "dp", scatter_dimension=0, tiled=True).astype(F32)
 
-        g_q, g_p, g_u, g_d = (scatter(g) for g in (g_q[:, : 3 * WIDE], g_p[:, :WIDE], g_u, g_d))
+        g_x, g_u, g_d = (scatter(g) for g in (g_x, g_u, g_d))
         vec = lax.psum(vec, "dp")
     image_result = img_out.reshape(images, rows_i, width)[:, :keys_i][None]
     text_result = txt_out.reshape(blocks, length, width)[None]
@@ -695,9 +738,9 @@
         text_result,
         vec[0:2][None],
         vec[2:4][None],
-        g_q[:, : 3 * WIDE].reshape(share, 3, WIDE)[None],
+        g_x[:, : 3 * WIDE].reshape(share, 3, WIDE)[None],
         jnp.stack([vec[8, 0:WIDE], vec[8, 2 * WIDE : 3 * WIDE]])[None],
-        g_p[:, :WIDE].T[None],
+        g_x[:, 3 * WIDE :].T[None],
         vec[4:6][None],
         g_u[None],
         vec[6][None],

time: 185 us -> 151 us (0.82)
  Pallas kernels: 158 us -> 124 us
    pallas_call x1, Pallas kernels: 158 us -> 124 us  [per_device(): pl.pallas_call(partial(layers_kernel, rows_i, rows_t, keys_i, dp_size, z_...]
    unnamed x17 -> x15, local copies, waits for them, and re-layouts: 8.27 us -> 8.27 us
where the time goes in v2:
time: 151 us
  Pallas kernels  124 us (82%)
  local copies, waits for them, and re-layouts  24.1 us (16%)
  other arithmetic  1.55 us (1%)
    pallas_call x1, Pallas kernels, per_device(): pl.pallas_call(partial(layers_kernel, rows_i, rows_t, keys_i, dp_size, z_...  124 us
    unnamed x15, local copies, waits for them, and re-layouts  8.27 us

profile of v2, /device:TPU:0, one launch (start us, length us, event | category | flops | bytes accessed | tf_op | source)
XLA Modules:
  0.0 150.6 jit_solution(16076499425167214394)
XLA Ops:
  0.6 0.0 copy-start
  0.7 0.8 fusion
  1.5 0.2 reduce-window.8
  1.7 0.1 convert_reduce_fusion
  1.8 0.8 fusion.2
  2.6 0.6 broadcast_in_dim.48.seg_row
  3.1 0.7 reduce
  3.9 0.1 concatenate.3
  3.9 0.6 broadcast_in_dim.46.small
  4.6 0.9 copy.36.seg_col
  5.4 2.1 %dynamic-slice_bitcast_fusion.txt_own = bf16[512,768]{1,0:T(8,128)(2,1)} fusion(bf16[1,2,512,768]{3,2,1,0:T(8,128)(2,1)} %param.13, s32[]{:T(128)S(6)} %select_n.8), kind=kLoop, calls=%fused_computation.2 | loop fusion | bytes 1572868 | tf_op jit(solution)/shard_map/squeeze | solution.py:682
  7.5 1.5 %copy.35 = bf16[768,576]{1,0:T(8,128)(2,1)S(1)} copy(bf16[768,576]{0,1:T(8,128)(2,1)} %bitcast.49) | data formatting | bytes 1769472 | tf_op jit(solution)/shard_map/reshape;squeeze | solution.py:688
  9.0 1.0 pad.13.w_qkv
  10.1 0.0 copy-done
  10.1 0.6 constant_dynamic-slice_fusion.1
  10.7 0.1 copy.46
  10.8 1.1 pad.12
  12.0 124.2 %shard_map.203 = (bf16[1664,768]{1,0:T(8,128)(2,1)}, bf16[1024,768]{1,0:T(8,128)(2,1)}, f32[192,768]{1,0:T(8,128)}, f32[192,768]{1,0:T(8,128)}, f32[192,768]{1,0:T(8,128)}, /*index=5*/f32[16,768]{1,0:T(8,128)}) custom-call(bf16[832,768]{1,0:T(8,128)(2,1)} %bitcast.41, bf16[512,768]{1,0:T(8,128)(2,1)} %dynamic-slice_bitcast_fusion.txt_own, ...), custom_call_target="tpu_custom_call" | custom-call | tf_op jit(solution)/shard_map/pallas_call | solution.py:718
  136.2 1.9 %slice.44 = bf16[8,197,768]{2,1,0:T(8,128)(2,1)S(1)} slice(bf16[8,208,768]{2,1,0:T(8,128)(2,1)} %bitcast.44), slice={[0:8], [0:197], [0:768]} | slice | bytes 4841472 | tf_op jit(solution)/shard_map/slice | solution.py:734
  138.0 1.9 %copy.45 = bf16[8,197,768]{2,0,1:T(8,128)(2,1)} copy(bf16[8,197,768]{2,1,0:T(8,128)(2,1)S(1)} %slice.44) | data formatting | bytes 4841472
  139.9 0.7 fusion.1
  140.6 0.6 maximum_bitcast_fusion
  141.2 1.3 slice.43
  142.6 1.5 slice_bitcast_fusion.1
  144.0 0.1 slice_bitcast_fusion
  144.2 0.8 copy.40
  145.0 0.2 copy.38
  145.2 1.1 copy.39
  146.3 2.7 %copy.50 = bf16[1,2,512,768]{3,2,1,0:T(8,128)(2,1)} copy(bf16[1,2,512,768]{3,2,1,0:T(8,128)(2,1)} %bitcast.46) | data formatting | bytes 3145728
  149.0 0.8 copy.51
  149.8 0.0 copy-done.2
  149.8 0.8 copy.52
  (9 shorter events, 0.1 us)
Async XLA Ops:
  0.6 9.4 %copy-start = (bf16[1,8,197,768]{3,1,2,0:T(8,128)(2,1)S(1)}, bf16[1,8,197,768]{3,1,2,0:T(8,128)(2,1)}, u32[]{:S(2)}) copy-start(bf16[1,8,197,768]{3,1,2,0:T(8,128)(2,1)} %param.12) | copy-start | bytes 7262212
  138.0 6.0 %copy-start.1 = (f32[192,768]{1,0:T(8,128)S(1)}, f32[192,768]{1,0:T(8,128)}, u32[]{:S(2)}) copy-start(f32[192,768]{1,0:T(8,128)} %get-tuple-element.20) | copy-start | bytes 1769476
  146.3 2.8 %copy-start.3 = (f32[192,768]{1,0:T(8,128)S(1)}, f32[192,768]{1,0:T(8,128)}, u32[]{:S(2)}) copy-start(f32[192,768]{1,0:T(8,128)} %get-tuple-element.21) | copy-start | bytes 1769476
  146.3 3.6 %copy-start.2 = (f32[192,768]{1,0:T(8,128)S(1)}, f32[192,768]{1,0:T(8,128)}, u32[]{:S(2)}) copy-start(f32[192,768]{1,0:T(8,128)} %get-tuple-element.22) | copy-start | bytes 1769476

commit v3 on v2

--- a/solution.py
+++ b/solution.py
@@ -18,6 +18,7 @@
 MASKED = -1000000000.0
 CHUNKS = 4
 STRIP = 16
+STEP = 64
 BLOCK = 208
 QKV = 640
 MIX = 256
@@ -73,9 +74,9 @@
 
 def layers_kernel(
     rows_i, rows_t, keys_i, dp_size, z_inside,
-    img_own, txt_own, w_qkv, w_proj, w_up, w_down, small, gains, shifts, outb, seg_col, seg_row,
+    img_own, txt_all, w_qkv, w_proj, w_up, w_down, lengths, gains, shifts, outb, bias_up, bias_qv,
     img_out, txt_out, g_mix, g_up, g_down, vec_out,
-    x_s, dy_s, wq_s, wp_s, wu_s, wd_s, small_s, a1_s, qkv_s, o_s, r_s, a2_s, gb_s, du_s, p_s, dkv_s, do_s,
+    x_s, dy_s, wq_s, wp_s, wu_s, wd_s, small_s, seg_s, a1_s, qkv_s, o_s, r_s, a2_s, gb_s, du_s, p_s, dkv_s, do_s,
     send_s, ra_s, rb_s, rc_s, ys_s, yt_s, y1_s, y2_s, fin_s, acc_s, vec_s, vrec_s, vall_s,
     gs_x, gs_u, gs_d, gr_x, gr_u, gr_d, *rest,
 ):
@@ -91,6 +92,7 @@
     other = 1 - p
     sib, peer = (p, d, sib_t), (p, d, peer_t)
     across = (other, d, t)
+    txt_own = txt_all.at[core]
     offsets = range(1, dp_size) if z_inside else range(0)
     partners = [sib, peer, across]
     partners += [(p, lax.rem(d + k, dp_size), t) for k in offsets]
@@ -109,14 +111,12 @@
     n_img = rows_i * CHUNKS
     n_txt = rows_t * CHUNKS
 
-    wq_own = local(w_qkv, wq_s.at[:, 0:QKV], 0)
+    wq_own = local(w_qkv, wq_s.at[0 : 3 * WIDE], 0)
     wp_own = local(w_proj, wp_s.at[PAD:MIX], 1)
     wu_own = local(w_up, wu_s.at[:, 0:width], 2)
     wd_own = local(w_down, wd_s.at[0:width], 3)
-    sm_own = local(small, small_s.at[0], 4)
     img_in = local(img_own, x_s, 5)
     txt_in = local(txt_own, dy_s.at[0:n_txt], 6)
-    sm_own.start()
     wq_own.start()
 
     @pl.when(image_here)
@@ -133,15 +133,22 @@
     zero_rows = jnp.zeros((PAD, width), BF16)
     wp_s[0:PAD, :] = zero_rows
     wp_s[MIX : MIX + PAD, :] = zero_rows
+    zero_rows = jnp.zeros((QKV - 3 * WIDE, width), BF16)
+    wq_s[3 * WIDE : QKV, :] = zero_rows
+    wq_s[QKV + 3 * WIDE :, :] = zero_rows
     acc_s[...] = jnp.zeros_like(acc_s)
+    small_s[0] = jnp.zeros_like(small_s[0])
+    small_s[0, 0:1, 0:width] = bias_up[...]
+    small_s[0, 0:1, width : width + WIDE] = bias_qv[0:1, :]
+    small_s[0, 0:1, width + 2 * WIDE : width + 3 * WIDE] = bias_qv[1:2, :]
 
     barrier = pltpu.get_barrier_semaphore()
     for to in partners:
         pl.semaphore_signal(barrier, inc=1, device_id=to, device_id_type=BY_MESH)
     pl.semaphore_wait(barrier, len(partners))
 
-    sm_sib = remote(small, small_s.at[1], K_S, 0, sib)
-    wq_sib = remote(w_qkv, wq_s.at[:, QKV:], K_W, 0, sib)
+    sm_sib = remote(small_s.at[0], small_s.at[1], K_S, 0, sib)
+    wq_sib = remote(w_qkv, wq_s.at[QKV : QKV + 3 * WIDE], K_W, 0, sib)
     wp_sib = remote(w_proj, wp_s.at[MIX + PAD :], K_W, 1, sib)
     wu_sib = remote(w_up, wu_s.at[:, width:], K_W, 2, sib)
     wd_sib = remote(w_down, wd_s.at[width:], K_W, 3, sib)
@@ -272,9 +279,18 @@
 
         wq_own.wait()
         wq_sib.wait()
-        sm_own.wait()
         sm_sib.wait()
+        def caption(places):
+            bound = lengths[core, 0]
+            segment = (places >= bound).astype(jnp.int32)
+            for k in range(1, lengths.shape[1]):
+                bound = bound + lengths[core, k]
+                segment = segment + (places >= bound).astype(jnp.int32)
+            return segment
+
         if text:
+            places = lax.broadcasted_iota(jnp.int32, (8, total + 2 * rows_t), 1) - rows_t
+            seg_s[...] = jnp.where(places < 0, -1, caption(places))
             txt_in.wait()
             pad = jnp.zeros((rows_t, 2 * QKV), BF16)
             qkv_s[0:rows_t, :] = pad
@@ -298,7 +314,7 @@
             lanes = lax.broadcasted_iota(jnp.int32, (1, QKV), 1)
             factor = jnp.where(lanes < WIDE, HEAD**-0.5, 1.0).astype(F32)
             for s in range(2):
-                value = dot(left, wq_s[:, s * QKV : (s + 1) * QKV])
+                value = dot_nt(left, wq_s[s * QKV : (s + 1) * QKV, :])
                 value = (value + small_s[s, 0:1, width : width + QKV]) * factor
                 qkv_s[q_rows(i), s * QKV : (s + 1) * QKV] = value.astype(BF16)
 
@@ -314,8 +330,8 @@
 
         def allowed(i):
             if text:
-                mine = seg_col[at_rows(i), 0:1]
-                keys = seg_row[0:1, pl.ds(pl.multiple_of(i * rows_t, 128), span)]
+                mine = caption(lax.broadcasted_iota(jnp.int32, (rows, 1), 0) + i * rows)
+                keys = seg_s[0:1, pl.ds(pl.multiple_of(i * rows_t, 128), span)]
                 return mine == keys
             return lax.broadcasted_iota(jnp.int32, (1, span), 1) < keys_i
 
@@ -474,7 +490,7 @@
                     v0 = 2 * WIDE + s * WIDE
                     dq_s[at_rows(i), k0 + WIDE : k0 + 2 * WIDE] = dkv_s[q_rows(i), v0 : v0 + WIDE].astype(BF16)
             grad = dq_s[at_rows(i), 0 : 2 * QKV]
-            send_s[at_rows(i), :] = dot_nt(grad, wq_s[...]).astype(BF16)
+            send_s[at_rows(i), :] = dot(grad, wq_s[...]).astype(BF16)
             swap(i, rc_s, K_C).start()
             for s in range(2):
                 acc_s[8 + s, :, 0:QKV] += fold(grad[:, s * QKV : (s + 1) * QKV].astype(F32))
@@ -664,6 +680,88 @@
         one_layer(True)
 
 
+def finish_kernel(
+    images, keys_i, rows_i, img_in, txt_in, g_x, g_u, g_d, vec,
+    img_out, txt_out, gains, shifts, qkv, bias_qv, proj, outb, up, bias_up, down,
+    buf, out_s, gx_s, qkv_s, txt_s, gu_s, gd_s, sem,
+):
+    plain = [(g_u, gu_s, up), (g_d, gd_s, down), (txt_in, txt_s, txt_out)]
+    fetch = [pltpu.make_async_copy(src, mid, sem.at[k]) for k, (src, mid, dst) in enumerate(plain)]
+    copies = [pltpu.make_async_copy(mid, dst, sem.at[5 + k]) for k, (src, mid, dst) in enumerate(plain)]
+    gx_in = pltpu.make_async_copy(g_x, gx_s, sem.at[3])
+    gx_in.start()
+    blocks = [(o, min(STEP, rows_i - o)) for o in range(0, rows_i, STEP)]
+    loads = [
+        pltpu.make_async_copy(img_in.at[:, o : o + n], buf.at[:, o : o + n], sem.at[8 + k])
+        for k, (o, n) in enumerate(blocks)
+    ]
+    for cp in loads:
+        cp.start()
+    for cp in fetch:
+        cp.start()
+    gains[...] = vec[0:2, :]
+    shifts[...] = vec[2:4, :]
+    outb[...] = vec[4:6, :]
+    bias_up[...] = vec[6:7, :]
+    bias_qv[0:1, :] = vec[8:9, 0:WIDE]
+    bias_qv[1:2, :] = vec[8:9, 2 * WIDE : 3 * WIDE]
+    gx_in.wait()
+    proj[...] = gx_s[:, 3 * WIDE :].T
+    for k in range(3):
+        qkv_s[k] = gx_s[:, k * WIDE : (k + 1) * WIDE]
+    q_out = pltpu.make_async_copy(qkv_s, qkv, sem.at[4])
+    q_out.start()
+    stores = []
+    for k, (o, n) in enumerate(blocks):
+        loads[k].wait()
+        rows = min(n, keys_i - o)
+        value = jnp.swapaxes(buf[:, o : o + n, :].astype(F32), 0, 1)
+        out_s[o : o + n] = value.astype(BF16)
+        cp = pltpu.make_async_copy(out_s.at[o : o + rows], img_out.at[o : o + rows], sem.at[16 + k])
+        cp.start()
+        stores.append(cp)
+        if k < len(fetch):
+            fetch[k].wait()
+            copies[k].start()
+    for cp in copies + [q_out] + stores:
+        cp.wait()
+
+
+def finish_outputs(images, keys_i, rows_i, img_out, txt_out, g_x, g_u, g_d, vec):
+    share, width = g_x.shape
+    sds, v = jax.ShapeDtypeStruct, pltpu.VMEM
+    any_spec, vmem_spec = pl.BlockSpec(memory_space=pl.ANY), pl.BlockSpec(memory_space=pltpu.VMEM)
+    outs = [
+        (sds((keys_i, images, width), BF16), any_spec),
+        (sds(txt_out.shape, BF16), any_spec),
+        (sds((2, width), F32), vmem_spec),
+        (sds((2, width), F32), vmem_spec),
+        (sds((3, share, WIDE), F32), any_spec),
+        (sds((2, WIDE), F32), vmem_spec),
+        (sds((WIDE, share), F32), vmem_spec),
+        (sds((2, width), F32), vmem_spec),
+        (sds((share, width), F32), any_spec),
+        (sds((1, width), F32), vmem_spec),
+        (sds((share, width), F32), any_spec),
+    ]
+    img, txt, gains, shifts, qkv, bias_qv, proj, outb, up, bias_up, down = pl.pallas_call(
+        partial(finish_kernel, images, keys_i, rows_i),
+        out_shape=[o[0] for o in outs],
+        in_specs=[any_spec] * 5 + [vmem_spec],
+        out_specs=[o[1] for o in outs],
+        scratch_shapes=[
+            v((images, rows_i, width), BF16), v((rows_i, images, width), BF16), v((share, width), F32),
+            v((3, share, WIDE), F32), v(txt_out.shape, BF16), v((share, width), F32), v((share, width), F32),
+            pltpu.SemaphoreType.DMA((24,)),
+        ],
+        compiler_params=pltpu.CompilerParams(vmem_limit_bytes=60 << 20),
+    )(img_out.reshape(images, rows_i, width), txt_out, g_x, g_u, g_d, vec)
+    return (
+        jnp.transpose(img, (1, 0, 2))[None], txt.reshape(2, -1, width)[None], gains[None], shifts[None],
+        jnp.transpose(qkv, (1, 0, 2))[None], bias_qv[None], proj[None], outb[None], up[None], bias_up, down.T[None],
+    )
+
+
 def per_device(
     image_side, text_side, caption_lengths, norm_gains, norm_shifts, w_qkv, bias_qv, w_proj, out_bias, w_up, bias_up, w_down,
 ):
@@ -679,17 +777,7 @@
 
     img = lax.dynamic_slice_in_dim(image_side[0], core * per_core, per_core, 0)
     img = jnp.pad(img, ((0, 0), (0, rows_i - keys_i), (0, 0))).reshape(per_core * rows_i, width)
-    txt = lax.dynamic_slice_in_dim(text_side[0], core, 1, 0)[0]
-    bounds = jnp.cumsum(lax.dynamic_slice_in_dim(caption_lengths, core, 1, 0)[0])
-    places = jnp.arange(length, dtype=jnp.int32)
-    segment = jnp.sum((places[:, None] >= bounds[None, :]).astype(jnp.int32), axis=1)
-    seg_col = segment[:, None]
-    seg_row = jnp.pad(segment, (rows_t, rows_t), constant_values=-1)[None]
-    wq = jnp.pad(w_qkv[0].reshape(width, 3 * WIDE), ((0, 0), (0, QKV - 3 * WIDE)))
-    lane = jnp.zeros((WIDE,), F32)
-    small = jnp.concatenate([bias_up[0], bias_qv[0, 0], lane, bias_qv[0, 1], jnp.zeros((QKV - 3 * WIDE,), F32)])
-    small = jnp.broadcast_to(small[None], (8, small.shape[0]))
-
+    wq = jnp.transpose(w_qkv[0], (1, 2, 0)).reshape(3 * WIDE, width)
     n_i, n_t = rows_i * CHUNKS, rows_t * CHUNKS
     columns = (width, width, width)
     sds = jax.ShapeDtypeStruct
@@ -700,8 +788,8 @@
     v = pltpu.VMEM
     scratch = [
         v((n_i, width), BF16), v((n_i, width), BF16),
-        v((width, 2 * QKV), BF16), v((2 * MIX, width), BF16), v((width, 2 * width), BF16), v((2 * width, width), BF16),
-        v((2, 8, width + QKV), F32),
+        v((2 * QKV, width), BF16), v((2 * MIX, width), BF16), v((width, 2 * width), BF16), v((2 * width, width), BF16),
+        v((2, 8, width + QKV), F32), v((8, n_t + 2 * rows_t), jnp.int32),
         v((n_i, width), BF16), v((max(n_i, n_t + 2 * rows_t), 2 * QKV), BF16), v((n_i, 2 * MIX), BF16), v((n_i, width), F32),
         v((n_i, width), BF16), v((n_i, 2 * width), BF16), v((n_i, 2 * width), BF16),
         v((CHUNKS * HEADS, max(rows_i, rows_t), max(-(-rows_i // 128) * 128, 3 * rows_t)), F32),
@@ -718,14 +806,17 @@
     img_out, txt_out, g_x, g_u, g_d, vec = pl.pallas_call(
         partial(layers_kernel, rows_i, rows_t, keys_i, dp_size, z_inside),
         out_shape=outs,
-        in_specs=[any_spec] * 7 + [vmem_spec] * 5,
+        in_specs=[any_spec] * 6 + [pl.BlockSpec(memory_space=pltpu.SMEM)] + [vmem_spec] * 5,
         out_specs=[any_spec] * 5 + [vmem_spec],
         scratch_shapes=scratch,
         compiler_params=pltpu.CompilerParams(collective_id=0, has_side_effects=True, vmem_limit_bytes=60 << 20),
     )(
-        img, txt, wq, w_proj[0], w_up[0], w_down[0], small, norm_gains[0], norm_shifts[0], out_bias[0], seg_col, seg_row,
+        img, text_side[0], wq, w_proj[0], w_up[0], w_down[0], caption_lengths,
+        norm_gains[0], norm_shifts[0], out_bias[0], bias_up, bias_qv[0],
     )
-    if not z_inside:
+    if z_inside:
+        return finish_outputs(images, keys_i, rows_i, img_out, txt_out, g_x, g_u, g_d, vec)
+    else:
         def scatter(grad):
             return lax.psum_scatter(grad, "dp", scatter_dimension=0, tiled=True).astype(F32)
 

time: 151 us -> 135 us (0.89)
  local copies, waits for them, and re-layouts: 24.1 us -> 3.56 us
  Pallas kernels: 124 us -> 130 us
  other arithmetic: 1.55 us -> 0 us
    pallas_call x0 -> x1, Pallas kernels: none -> 6.52 us  [finish_outputs(): pl.pallas_call(partial(finish_kernel, images, keys_i, rows_i), out_shape=...]
    unnamed x15 -> x3, local copies, waits for them, and re-layouts: 8.27 us -> 1.8 us
    slice x6 -> x0, local copies, waits for them, and re-layouts: 4.9 us -> none  [the longest x1 1.86 us: per_device(): image_result = img_out.reshape(images, rows_i, width)[:, :keys_i][None]]
    broadcast_in_dim x7 -> x0, local copies, waits for them, and re-layouts: 3.63 us -> none  [the longest x1 1.46 us: per_device(): vec[4:6][None]]
    another operation x2 -> x0, local copies, waits for them, and re-layouts: 2.37 us -> none  [the longest x1 1.53 us: per_device(): w_qkv[0].reshape(width, 3 * WIDE)]
    squeeze x1 -> x0, local copies, waits for them, and re-layouts: 2.07 us -> none  [per_device(): txt = lax.dynamic_slice_in_dim(text_side[0], core, 1, 0)[0]]
where the time goes in v3:
time: 135 us
  Pallas kernels  130 us (96%)
  local copies, waits for them, and re-layouts  3.56 us (3%)
    pallas_call x1, Pallas kernels, per_device(): pl.pallas_call(partial(layers_kernel, rows_i, rows_t, keys_i, dp_size, z_...  124 us
    pallas_call x1, Pallas kernels, finish_outputs(): pl.pallas_call(partial(finish_kernel, images, keys_i, rows_i), out_shape=...  6.52 us

profile of v3, /device:TPU:0, one launch (start us, length us, event | category | flops | bytes accessed | tf_op | source)
XLA Modules:
  0.0 134.9 jit_solution(12114260003712718348)
XLA Ops:
  0.6 0.0 copy-start
  0.7 1.7 %copy-done = bf16[1,8,197,768]{3,1,2,0:T(8,128)(2,1)S(1)} copy-done((bf16[1,8,197,768]{3,1,2,0:T(8,128)(2,1)S(1)}, bf16[1,8,197,768]{3,1,2,0:T(8,128)(2,1)}, u32[]{:S(2)}) %copy-start) | copy-done | bytes 2420760
  2.3 0.6 constant_dynamic-slice_fusion
  3.0 0.1 copy.26
  3.1 1.1 pad.4
  4.2 123.9 %shard_map.203 = (bf16[1664,768]{1,0:T(8,128)(2,1)}, bf16[1024,768]{1,0:T(8,128)(2,1)}, f32[192,768]{1,0:T(8,128)}, f32[192,768]{1,0:T(8,128)}, f32[192,768]{1,0:T(8,128)}, /*index=5*/f32[16,768]{1,0:T(8,128)}) custom-call(bf16[832,768]{1,0:T(8,128)(2,1)} %bitcast.34, bf16[2,512,768]{2,1,0:T(8,128)(2,1)} %bitcast.37, bf16[576,768]{1,0:T(8,128)(2,1)} %bitcast.40, ...), custom_call_target="tpu_custom_call" | custom-call | tf_op jit(solution)/shard_map/pallas_call | solution.py:806
  128.2 6.5 %shard_map.204 = (bf16[197,8,768]{2,1,0:T(8,128)(2,1)}, bf16[1024,768]{1,0:T(8,128)(2,1)}, f32[2,768]{1,0:T(2,128)}, f32[2,768]{1,0:T(2,128)}, f32[3,192,192]{2,...) custom-call(bf16[8,208,768]{2,1,0:T(8,128)(2,1)} %bitcast.36, ...), custom_call_target="tpu_custom_call" | custom-call | tf_op jit(solution)/shard_map/pallas_call | solution.py:747
Async XLA Ops:
  0.6 1.7 %copy-start = (bf16[1,8,197,768]{3,1,2,0:T(8,128)(2,1)S(1)}, bf16[1,8,197,768]{3,1,2,0:T(8,128)(2,1)}, u32[]{:S(2)}) copy-start(bf16[1,8,197,768]{3,1,2,0:T(8,128)(2,1)} %param.12) | copy-start | bytes 7262212

commit v4 on v3

--- a/solution.py
+++ b/solution.py
@@ -18,6 +18,8 @@
 MASKED = -1000000000.0
 CHUNKS = 4
 STRIP = 16
+TURNS = 4
+G_TILE = 256
 STEP = 64
 BLOCK = 208
 QKV = 640
@@ -25,8 +27,10 @@
 PAD = MIX - WIDE
 TILE = 256
 
-K_IN, K_A, K_B, K_C, K_Y1, K_Y2, K_YT, K_OI, K_OT, K_T1, K_W, K_S, K_G, K_V, K_Z = range(15)
-N_KINDS = K_Z + 3
+K_IN, K_A, K_B, K_C, K_Y1, K_Y2, K_YT, K_OI, K_OT, K_T1, K_W, K_S, K_G, K_Z = range(14)
+K_V = K_Z + 3
+K_E = K_V + 2
+N_KINDS = K_E + 1
 
 
 def dot(a, b):
@@ -77,8 +81,8 @@
     img_own, txt_all, w_qkv, w_proj, w_up, w_down, lengths, gains, shifts, outb, bias_up, bias_qv,
     img_out, txt_out, g_mix, g_up, g_down, vec_out,
     x_s, dy_s, wq_s, wp_s, wu_s, wd_s, small_s, seg_s, a1_s, qkv_s, o_s, r_s, a2_s, gb_s, du_s, p_s, dkv_s, do_s,
-    send_s, ra_s, rb_s, rc_s, ys_s, yt_s, y1_s, y2_s, fin_s, acc_s, vec_s, vrec_s, vall_s,
-    gs_x, gs_u, gs_d, gr_x, gr_u, gr_d, *rest,
+    send_s, ra_s, rb_s, rc_s, ys_s, yt_s, y1_s, y2_s, fin_s, acc_s, early_s, esib_s, eall_s, late_s, lall_s,
+    half_s, gs_x, gs_u, gs_d, gr_x, gr_u, gr_d, *rest,
 ):
     if z_inside:
         z1_s, z2_s, zf_s, ssem, rsem, lsem = rest
@@ -93,9 +97,14 @@
     sib, peer = (p, d, sib_t), (p, d, peer_t)
     across = (other, d, t)
     txt_own = txt_all.at[core]
-    offsets = range(1, dp_size) if z_inside else range(0)
-    partners = [sib, peer, across]
-    partners += [(p, lax.rem(d + k, dp_size), t) for k in offsets]
+    groups = dp_size if z_inside else 1
+    adders = [(k, j) for k in range(groups) for j in range(2) if k + j > 0]
+
+    def adder(k, j, back=False):
+        dist = dp_size - k if back else k
+        return (p, lax.rem(d + dist, dp_size) if k else d, sib_t if j else t)
+
+    partners = [peer, across] + [adder(k, j) for k, j in adders]
 
     def remote(src, dst, kind, slot, to):
         at = kind * 4 + slot
@@ -145,6 +154,18 @@
     barrier = pltpu.get_barrier_semaphore()
     for to in partners:
         pl.semaphore_signal(barrier, inc=1, device_id=to, device_id_type=BY_MESH)
+
+    @pl.when(image_here)
+    def _():
+        img_in.wait()
+
+        def first_norm(i):
+            at = pl.ds(pl.multiple_of(i * rows_i, 16), rows_i)
+            unit, _ = unit_of(x_s[at, :].astype(F32))
+            a1_s[at, :] = (unit * gains[0:1, :] + shifts[0:1, :]).astype(BF16)
+
+        loop(CHUNKS, first_norm)
+
     pl.semaphore_wait(barrier, len(partners))
 
     sm_sib = remote(small_s.at[0], small_s.at[1], K_S, 0, sib)
@@ -182,29 +203,29 @@
     g_arrays = [(gs_x, gr_x, g_mix), (gs_u, gr_u, g_up), (gs_d, gr_d, g_down)]
 
     def g_exchange(a):
-        return remote(g_arrays[a][0], g_arrays[a][1], K_G, a, sib)
-
-    def grads_pair(a, product):
+        return remote(half_s.at[a % 2], g_arrays[a][1], K_G, a, sib)
+
+    def grads_part(a, product, first):
+        mine, theirs = g_arrays[a][0], half_s.at[a % 2]
+
+        def both(m):
+            at = pl.ds(pl.multiple_of(m * G_TILE, G_TILE), G_TILE)
+            for ref, value in zip((mine, theirs), product(at)):
+                ref[at, :] = (value if first else value + ref[at, :].astype(F32)).astype(BF16)
+
+        loop(width // G_TILE, both)
+        if not first:
+            g_exchange(a).start()
+
+    def grads_sum(a):
+        g_exchange(a).wait()
         mine, theirs = g_arrays[a][0:2]
-        tiles = width // TILE
-
-        def send_half(m):
-            at = pl.ds(pl.multiple_of(m * TILE, TILE), TILE)
-            mine[at, :] = product(at, 1).astype(BF16)
-
-        loop(tiles, send_half)
-        g_exchange(a).start()
-
-        def finish():
-            g_exchange(a).wait()
-
-            def own_half(m):
-                at = pl.ds(pl.multiple_of(m * TILE, TILE), TILE)
-                mine[at, :] = (product(at, 0) + theirs[at, :].astype(F32)).astype(BF16)
-
-            loop(tiles, own_half)
-
-        return finish
+
+        def body(m):
+            at = pl.ds(pl.multiple_of(m * G_TILE, G_TILE), G_TILE)
+            mine[at, :] = (mine[at, :].astype(F32) + theirs[at, :].astype(F32)).astype(BF16)
+
+        loop(width // G_TILE, body)
 
     share = width // dp_size
     parity = lax.rem(d, 2)
@@ -224,15 +245,13 @@
 
     def z_start(a):
         if z_inside:
-            for k in range(2):
-                z_near(a, k).start()
+            z_near(a, 1 - upper).start()
         else:
             local(g_arrays[a][0], g_arrays[a][2], 20 + a).start()
 
     def z_middle(a):
         if z_inside:
-            for k in range(2):
-                z_near(a, k).wait()
+            z_near(a, 1 - upper).wait()
             mine = g_arrays[a][0]
             rows = share_rows(far)
             mine[rows, :] = (mine[rows, :].astype(F32) + z1_s[a, 1 - upper].astype(F32)).astype(BF16)
@@ -240,6 +259,7 @@
 
     def z_finish(a):
         if z_inside:
+            z_near(a, upper).wait()
             z_far(a).wait()
             total = g_arrays[a][0][share_rows(d), :].astype(F32) + z1_s[a, upper].astype(F32)
             zf_s[a] = total + z2_s[a].astype(F32)
@@ -296,8 +316,6 @@
             qkv_s[0:rows_t, :] = pad
             qkv_s[rows_t + total : 2 * rows_t + total, :] = pad
             dkv_s[...] = jnp.zeros_like(dkv_s)
-        else:
-            img_in.wait()
         for s in range(2):
             o_s[0:total, s * MIX : s * MIX + PAD] = jnp.zeros((total, PAD), BF16)
 
@@ -309,7 +327,8 @@
                 unit, _ = unit_of(x_s[at, :].astype(F32))
                 a1_s[at, :] = (unit * own_gain[0] + own_shift[0]).astype(BF16)
 
-            by_strips(i, first_norm)
+            if text:
+                by_strips(i, first_norm)
             left = a1_s[at_rows(i), :]
             lanes = lax.broadcasted_iota(jnp.int32, (1, QKV), 1)
             factor = jnp.where(lanes < WIDE, HEAD**-0.5, 1.0).astype(F32)
@@ -324,6 +343,15 @@
             return slice(base, base + HEAD), slice(base + WIDE, base + WIDE + HEAD), slice(base + 2 * WIDE, base + 2 * WIDE + HEAD), slice(s * MIX + PAD + hh * HEAD, s * MIX + PAD + hh * HEAD + HEAD)
 
         span = 3 * rows_t if text else rows_i
+        pieces = [(o, min(128, span - o)) for o in range(0, span, 128)]
+
+        def keep_weights(at, value):
+            for k, (o, n) in enumerate(pieces):
+                p_s[at, k * rows : (k + 1) * rows, 0:n] = value[:, o : o + n]
+
+        def kept_weights(at):
+            parts = [p_s[at, k * rows : (k + 1) * rows, 0:n] for k, (o, n) in enumerate(pieces)]
+            return jnp.concatenate(parts, axis=1)
 
         def key_rows(i):
             return pl.ds(pl.multiple_of(i * rows, 16), span)
@@ -343,7 +371,7 @@
                 scores = jnp.where(ok, scores, MASKED)
                 raised = jnp.exp(scores - jnp.max(scores, axis=-1, keepdims=True))
                 weights = raised * (1.0 / jnp.sum(raised, axis=-1, keepdims=True))
-                p_s[i * HEADS + h, 0:rows, 0:span] = weights
+                keep_weights(i * HEADS + h, weights)
                 mixed = dot(weights.astype(BF16), qkv_s[key_rows(i), vc])
                 o_s[at_rows(i), oc] = mixed.astype(BF16)
 
@@ -394,14 +422,37 @@
                 return [remote(ys_s.at[at], yt_s.at[at], K_YT, i, peer)]
             return [remote(ys_s.at[at], y1_s.at[at], K_Y1, i, across)]
 
-        def y_relay(i):
+        def owned(i):
+            return lax.rem(i, 2) == t // 2
+
+        def y_side(i):
             at = pl.ds(pl.multiple_of(i * rows_i, 16), rows_i)
-            return remote(y1_s.at[at], y2_s.at[at], K_Y2, i, peer)
+            there = y1_s if text and i < TURNS else y2_s
+            return remote((y1_s if text else ys_s).at[at], there.at[at], K_Y2, i, peer)
+
+        def y_share(i):
+            @pl.when(jnp.logical_not(owned(i)))
+            def _():
+                y_side(i).start()
+
+        def y_sum(i):
+            @pl.when(owned(i))
+            def _():
+                y_side(i).wait_recv()
+                at = at_rows(i)
+                ys_s[at, :] = (ys_s[at, :].astype(F32) + y2_s[at, :].astype(F32)).astype(BF16)
+                y_copies(i)[0].start()
 
         def hand_on(i):
-            at = pl.ds(pl.multiple_of(i * rows_i, 16), rows_i)
-            remote(y1_s.at[at], y1_s.at[at], K_Y1, i, across).wait_recv()
-            y_relay(i).start()
+            def go():
+                at = pl.ds(pl.multiple_of(i * rows_i, 16), rows_i)
+                remote(y1_s.at[at], y1_s.at[at], K_Y1, i, across).wait_recv()
+                y_side(i).start()
+
+            if i < TURNS:
+                pl.when(owned(i))(go)
+            else:
+                go()
 
         def middle(i):
             if not text:
@@ -432,16 +483,40 @@
             lower = dot(gb_s[at_rows(i), :], wd_s[...])
             ys_s[at_rows(i), :] = (lower + 0.5 * (r_s[at_rows(i), :] + outb[1:2, :])).astype(BF16)
             if not text:
-                for cp in y_copies(i):
-                    cp.start()
-
-        loop(CHUNKS, middle)
-        end_d = grads_pair(2, lambda at, s: dot_tn(dy_s[0:total, at], gb_s[0:total, s * width : (s + 1) * width]))
-        end_u = grads_pair(1, lambda at, s: dot_tn(a2_s[0:total, at], du_s[0:total, s * width : (s + 1) * width]))
-        end_d()
+
+                @pl.when(i >= TURNS)
+                def _():
+                    y_copies(i)[0].start()
+        parts = (slice(0, total // 2), slice(total // 2, total))
+
+        def halves(left, right, part):
+            def product(at):
+                value = dot_tn(left[part, at], right[part, :])
+                return value[:, :width], value[:, width:]
+
+            return product
+
+        def middle_and_grads(i):
+            middle(i)
+
+            @pl.when(i == 1)
+            def _():
+                grads_part(2, halves(dy_s, gb_s, parts[0]), True)
+
+            @pl.when(i == 2)
+            def _():
+                grads_part(1, halves(a2_s, du_s, parts[0]), True)
+
+        loop(CHUNKS, middle_and_grads)
+        grads_part(2, halves(dy_s, gb_s, parts[1]), False)
+        grads_part(1, halves(a2_s, du_s, parts[1]), False)
+        grads_sum(2)
         z_start(2)
-        end_u()
+        grads_sum(1)
         z_start(1)
+        if z_inside:
+            z_near(2, upper).start()
+            z_near(1, upper).start()
 
         dq_s, drb_s = gb_s, a2_s
         for s in range(2):
@@ -464,7 +539,7 @@
             do_s[0:rows, :] = dot_nt(drb_s[at_rows(i), :], wp_s[...]).astype(BF16)
             for h in range(HEADS):
                 qc, kc, vc, oc = head_at(h)
-                weights = p_s[i * HEADS + h, 0:rows, 0:span]
+                weights = kept_weights(i * HEADS + h)
                 grad_o = do_s[0:rows, oc]
                 keys = qkv_s[key_rows(i), kc]
                 slope = dot_nt(grad_o, qkv_s[key_rows(i), vc])
@@ -502,7 +577,7 @@
             return txt_out.at[pl.ds(pl.multiple_of(core * n_txt + i * rows_t, 16), rows_t)]
 
         def img_copies(i):
-            src = fin_s.at[pl.ds(pl.multiple_of(i * rows_i, 16), rows_i)]
+            src = (y1_s if text else fin_s).at[pl.ds(pl.multiple_of(i * rows_i, 16), rows_i)]
             return local(src, own_img(i), 8 + i), remote(src, own_img(i), K_OI, i, sib)
 
         def txt_copies(i):
@@ -527,8 +602,19 @@
 
             def image_y(i):
                 at = pl.ds(pl.multiple_of(i * rows_i, 16), rows_i)
-                y_relay(i).wait()
-                fin_s[at, :] = (y1_s[at, :].astype(F32) + y2_s[at, :].astype(F32)).astype(BF16)
+                if i < TURNS:
+
+                    @pl.when(owned(i))
+                    def _():
+                        y_side(i).wait_send()
+
+                    @pl.when(jnp.logical_not(owned(i)))
+                    def _():
+                        y_side(i).wait_recv()
+
+                else:
+                    y_side(i).wait()
+                    y1_s[at, :] = (y1_s[at, :].astype(F32) + y2_s[at, :].astype(F32)).astype(BF16)
                 for cp in img_copies(i):
                     cp.start()
 
@@ -551,9 +637,84 @@
             for cp in [dx_copies(i)] if text else img_copies(i):
                 cp.start()
 
-        if text:
-            hand_on(0)
-            hand_on(1)
+        if not text:
+            for i in range(TURNS):
+                y_share(i)
+        def mixed_grads(part):
+            def product(at):
+                first = dot_tn(a1_s[part, at], dq_s[part, 0 : 2 * QKV])
+                second = dot_tn(drb_s[part, at], o_s[part, :])
+
+                def joined(s):
+                    left, right = first[:, s * QKV : (s + 1) * QKV], second[:, s * MIX : (s + 1) * MIX]
+                    seam = left[:, MIX * 2 :] + right[:, 0 : QKV - 2 * MIX]
+                    return jnp.concatenate([left[:, : MIX * 2], seam, right[:, QKV - 2 * MIX :]], axis=1)
+
+                return joined(0), joined(1)
+
+            return product
+
+        group = d if z_inside else 0
+
+        def early_copy(k):
+            return remote(early_s.at[0], eall_s.at[group], K_E, k - 1, adder(k, 0))
+
+        def early_arrival(k):
+            place = lax.rem(d + dp_size - k, dp_size)
+            return remote(eall_s.at[place], eall_s.at[place], K_E, k - 1, adder(k, 0, True))
+
+        early_sib = remote(early_s.at[1], esib_s, K_S, 1, sib)
+
+        def early_start():
+            sums = jnp.sum(acc_s[...], axis=1)
+            for j, order in enumerate(((1, 3, 4, 5, 6, 7, 8, 9), (1, 3, 4, 5, 7, 6, 9, 8))):
+                for row, src in enumerate(order):
+                    early_s[j, row : row + 1, :] = sums[src : src + 1, :]
+            early_sib.start()
+
+        def early_next():
+            early_sib.wait()
+            early_s[0] = early_s[0] + esib_s[...]
+            eall_s[group] = early_s[0]
+            for k in range(1, groups):
+                early_copy(k).start()
+
+        def late_copy(k, j):
+            return remote(late_s, lall_s.at[2 * group + core], K_V, 2 * k + j, adder(k, j))
+
+        def late_arrival(k, j):
+            place = 2 * (lax.rem(d + dp_size - k, dp_size) if k else group) + (1 - core if j else core)
+            return remote(lall_s.at[place], lall_s.at[place], K_V, 2 * k + j, adder(k, j, True))
+
+        def late_start():
+            late_s[...] = jnp.zeros_like(late_s)
+            for r, src in enumerate((0, 2)):
+                row = jnp.sum(acc_s[src], axis=0, keepdims=True)
+                for c in range(width // 128):
+                    late_s[8 * r + c : 8 * r + c + 1, :] = row[:, c * 128 : (c + 1) * 128]
+            for k, j in adders:
+                late_copy(k, j).start()
+            lall_s[2 * group + core] = late_s[...]
+
+        def vectors_finish():
+            for k in range(1, groups):
+                early_copy(k).wait_send()
+                early_arrival(k).wait_recv()
+            for k, j in adders:
+                late_copy(k, j).wait_send()
+                late_arrival(k, j).wait_recv()
+            early, late = eall_s[0], lall_s[0]
+            for k in range(1, groups):
+                early = early + eall_s[k]
+            for k in range(1, 2 * groups):
+                late = late + lall_s[k]
+            vec_out[...] = jnp.zeros_like(vec_out)
+            for row, dst in enumerate((1, 3, 4, 5, 6, 7, 8, 9)):
+                vec_out[dst : dst + 1, :] = early[row : row + 1, :]
+            for r, dst in enumerate((0, 2)):
+                for c in range(width // 128):
+                    vec_out[dst : dst + 1, c * 128 : (c + 1) * 128] = late[8 * r + c : 8 * r + c + 1, :]
+
         if text:
 
             def backward(i):
@@ -561,13 +722,21 @@
                 def _():
                     attend_back(i)
 
-                @pl.when(i == CHUNKS - 1)
+                @pl.when(i == 2)
                 def _():
                     z_middle(2)
 
+                @pl.when(i == 3)
+                def _():
+                    z_middle(1)
+
                 @pl.when(i > 0)
                 def _():
                     send_c(i - 1)
+
+                @pl.when(i == 3)
+                def _():
+                    grads_part(0, mixed_grads(parts[0]), True)
 
                 @pl.when(i > 2)
                 def _():
@@ -577,76 +746,59 @@
         else:
 
             def backward(i):
-                @pl.when(i == CHUNKS - 1)
+                @pl.when(i == 2)
                 def _():
                     z_middle(2)
+
+                @pl.when(i == 3)
+                def _():
+                    z_middle(1)
 
                 attend_back(i)
                 send_c(i)
 
+                @pl.when(i == 2)
+                def _():
+                    grads_part(0, mixed_grads(parts[0]), True)
+
             loop(CHUNKS, backward)
 
-        def mixed_grads(at, s):
-            first = dot_tn(a1_s[0:total, at], dq_s[0:total, s * QKV : (s + 1) * QKV])
-            second = dot_tn(drb_s[0:total, at], o_s[0:total, s * MIX : (s + 1) * MIX])
-            seam = first[:, MIX * 2 :] + second[:, 0 : QKV - 2 * MIX]
-            return jnp.concatenate([first[:, : MIX * 2], seam, second[:, QKV - 2 * MIX :]], axis=1)
 
         if text:
+            for i in range(TURNS, CHUNKS):
+                hand_on(i)
             loop(CHUNKS, lambda i: y_copies(i)[0].start())
-        end_x = grads_pair(0, mixed_grads)
-        end_x()
+        grads_part(0, mixed_grads(parts[1]), False)
+        grads_sum(0)
         z_start(0)
+        if z_inside:
+            z_near(0, upper).start()
+        early_start()
         if text:
             last(CHUNKS - 2)
             last(CHUNKS - 1)
-            hand_on(2)
-            hand_on(3)
-            z_middle(1)
+            early_next()
+            z_middle(0)
+            for i in range(TURNS):
+                hand_on(i)
             loop(CHUNKS, own_y)
+        else:
+            for i in range(TURNS):
+                y_sum(i)
+            loop(2, last)
+            early_next()
             z_middle(0)
-        else:
-            z_middle(1)
-            loop(CHUNKS - 1, last)
-            z_middle(0)
+            last(CHUNKS - 2)
             last(CHUNKS - 1)
 
-
-        order = (0, 1, 2, 3, 4, 5, 7, 6, 9, 8, 10, 11, 12, 13, 14, 15)
-        sums = jnp.sum(acc_s[...], axis=1)
-        vec_s[0] = sums
-        for row, src in enumerate(order):
-            vec_s[1, row : row + 1, :] = sums[src : src + 1, :]
-        v_sib = remote(vec_s.at[1], vrec_s, K_S, 1, sib)
-        v_sib.start()
+        late_start()
         z_finish(2)
         z_finish(1)
-        v_sib.wait()
-        vec_s[0] = vec_s[0] + vrec_s[...]
-        if z_inside:
-            vall_s[d] = vec_s[0]
-
-            def v_copy(k):
-                to = lax.rem(d + k, dp_size)
-                return remote(vec_s.at[0], vall_s.at[d], K_V, k - 1, (p, to, t))
-
-            for k in offsets:
-                v_copy(k).start()
         if text:
-            loop(CHUNKS, image_y)
+            for i in range(CHUNKS):
+                image_y(i)
         z_finish(0)
-        if z_inside:
-            for k in offsets:
-                v_copy(k).wait_send()
-            for k in offsets:
-                back = lax.rem(d + dp_size - k, dp_size)
-                remote(vall_s.at[back], vall_s.at[back], K_V, k - 1, (p, back, t)).wait_recv()
-            totals = vall_s[0]
-            for k in range(1, dp_size):
-                totals = totals + vall_s[k]
-            vec_out[...] = totals
-        else:
-            vec_out[...] = vec_s[0]
+        vectors_finish()
 
         def finish(i):
             if text:
@@ -657,15 +809,26 @@
                 there.wait()
             else:
                 x_to_text(i).wait_send()
-                for cp in y_copies(i):
-                    cp.wait_send()
+                if i < TURNS:
+
+                    @pl.when(owned(i))
+                    def _():
+                        y_copies(i)[0].wait_send()
+
+                    @pl.when(jnp.logical_not(owned(i)))
+                    def _():
+                        y_side(i).wait_send()
+
+                else:
+                    y_copies(i)[0].wait_send()
                 dx_copies(i).wait_recv()
                 dx_relay(i).start()
             here, there = img_copies(i)
             here.wait()
             there.wait()
 
-        loop(CHUNKS, finish)
+        for i in range(CHUNKS):
+            finish(i)
         if not text:
             loop(CHUNKS, lambda i: dx_relay(i).wait())
         for a in range(3):
@@ -792,12 +955,14 @@
         v((2, 8, width + QKV), F32), v((8, n_t + 2 * rows_t), jnp.int32),
         v((n_i, width), BF16), v((max(n_i, n_t + 2 * rows_t), 2 * QKV), BF16), v((n_i, 2 * MIX), BF16), v((n_i, width), F32),
         v((n_i, width), BF16), v((n_i, 2 * width), BF16), v((n_i, 2 * width), BF16),
-        v((CHUNKS * HEADS, max(rows_i, rows_t), max(-(-rows_i // 128) * 128, 3 * rows_t)), F32),
+        v((CHUNKS * HEADS, max(-(-rows_i // 128) * rows_i, 3 * rows_t // 128 * rows_t), 128), F32),
         v((n_t + 2 * rows_t, 2 * HEADS * HEAD), F32), v((max(rows_i, rows_t), 2 * MIX), BF16),
         v((n_i, width), BF16), v((n_i, width), BF16), v((n_i, width), BF16), v((n_i, width), BF16),
         v((n_i, width), BF16), v((n_t, width), BF16), v((n_i, width), BF16), v((n_i, width), BF16), v((n_i, width), BF16),
-        v((16, 8, width), F32), v((2, 16, width), F32), v((16, width), F32), v((dp_size if z_inside else 1, 16, width), F32),
+        v((16, 8, width), F32), v((2, 8, width), F32), v((8, width), F32), v((dp_size if z_inside else 1, 8, width), F32),
+        v((16, 128), F32), v((2 * dp_size if z_inside else 2, 16, 128), F32),
     ]
+    scratch += [v((2, width, width), BF16)]
     scratch += [v((width, w), BF16) for w in columns] + [v((width, w), BF16) for w in columns]
     if z_inside:
         scratch += [v((3, 2, share, width), BF16), v((3, share, width), BF16), v((3, share, width), F32)]

time: 135 us -> 129 us (0.956)
  Pallas kernels: 130 us -> 125 us
    pallas_call x1, Pallas kernels: 124 us -> 118 us  [per_device(): pl.pallas_call(partial(layers_kernel, rows_i, rows_t, keys_i, dp_size, z_...]
where the time goes in v4:
time: 129 us
  Pallas kernels  125 us (97%)
  local copies, waits for them, and re-layouts  3.56 us (3%)
    pallas_call x1, Pallas kernels, per_device(): pl.pallas_call(partial(layers_kernel, rows_i, rows_t, keys_i, dp_size, z_...  118 us
    pallas_call x1, Pallas kernels, finish_outputs(): pl.pallas_call(partial(finish_kernel, images, keys_i, rows_i), out_shape=...  6.52 us

profile of v4, /device:TPU:0, one launch (start us, length us, event | category | flops | bytes accessed | tf_op | source)
XLA Modules:
  0.0 129.1 jit_solution(2528805577512929459)
XLA Ops:
  0.6 0.0 copy-start
  0.7 1.7 %copy-done = bf16[1,8,197,768]{3,1,2,0:T(8,128)(2,1)S(1)} copy-done((bf16[1,8,197,768]{3,1,2,0:T(8,128)(2,1)S(1)}, bf16[1,8,197,768]{3,1,2,0:T(8,128)(2,1)}, u32[]{:S(2)}) %copy-start) | copy-done | bytes 2420760
  2.3 0.6 constant_dynamic-slice_fusion
  3.0 0.1 copy.26
  3.1 1.1 pad.4
  4.2 118.2 %shard_map.203 = (bf16[1664,768]{1,0:T(8,128)(2,1)}, bf16[1024,768]{1,0:T(8,128)(2,1)}, f32[192,768]{1,0:T(8,128)}, f32[192,768]{1,0:T(8,128)}, f32[192,768]{1,0:T(8,128)}, /*index=5*/f32[16,768]{1,0:T(8,128)}) custom-call(bf16[832,768]{1,0:T(8,128)(2,1)} %bitcast.34, bf16[2,512,768]{2,1,0:T(8,128)(2,1)} %bitcast.37, bf16[576,768]{1,0:T(8,128)(2,1)} %bitcast.40, ...), custom_call_target="tpu_custom_call" | custom-call | tf_op jit(solution)/shard_map/pallas_call | solution.py:971
  122.5 6.5 %shard_map.204 = (bf16[197,8,768]{2,1,0:T(8,128)(2,1)}, bf16[1024,768]{1,0:T(8,128)(2,1)}, f32[2,768]{1,0:T(2,128)}, f32[2,768]{1,0:T(2,128)}, f32[3,192,192]{2,...) custom-call(bf16[8,208,768]{2,1,0:T(8,128)(2,1)} %bitcast.36, ...), custom_call_target="tpu_custom_call" | custom-call | tf_op jit(solution)/shard_map/pallas_call | solution.py:910
Async XLA Ops:
  0.6 1.7 %copy-start = (bf16[1,8,197,768]{3,1,2,0:T(8,128)(2,1)S(1)}, bf16[1,8,197,768]{3,1,2,0:T(8,128)(2,1)}, u32[]{:S(2)}) copy-start(bf16[1,8,197,768]{3,1,2,0:T(8,128)(2,1)} %param.12) | copy-start | bytes 7262212

commit v5 on v4

--- a/solution.py
+++ b/solution.py
@@ -18,7 +18,7 @@
 MASKED = -1000000000.0
 CHUNKS = 4
 STRIP = 16
-TURNS = 4
+TURNS = 2
 G_TILE = 256
 STEP = 64
 BLOCK = 208
@@ -27,7 +27,8 @@
 PAD = MIX - WIDE
 TILE = 256
 
-K_IN, K_A, K_B, K_C, K_Y1, K_Y2, K_YT, K_OI, K_OT, K_T1, K_W, K_S, K_G, K_Z = range(14)
+K_IN, K_A, K_B, K_C, K_Y1, K_Y2, K_YT, K_OI, K_OT, K_T1, K_W, K_S, K_G = range(13)
+K_Z = K_G + 3
 K_V = K_Z + 3
 K_E = K_V + 2
 N_KINDS = K_E + 1
@@ -202,26 +203,27 @@
 
     g_arrays = [(gs_x, gr_x, g_mix), (gs_u, gr_u, g_up), (gs_d, gr_d, g_down)]
 
-    def g_exchange(a):
-        return remote(half_s.at[a % 2], g_arrays[a][1], K_G, a, sib)
-
-    def grads_part(a, product, first):
+    def g_exchange(a, m):
+        at = pl.ds(pl.multiple_of(m * G_TILE, G_TILE), G_TILE)
+        return remote(half_s.at[a % 2, at], g_arrays[a][1].at[at], K_G + m, a, sib)
+
+    def grads_part(a, product, first, final):
         mine, theirs = g_arrays[a][0], half_s.at[a % 2]
 
         def both(m):
             at = pl.ds(pl.multiple_of(m * G_TILE, G_TILE), G_TILE)
             for ref, value in zip((mine, theirs), product(at)):
                 ref[at, :] = (value if first else value + ref[at, :].astype(F32)).astype(BF16)
+            if final:
+                g_exchange(a, m).start()
 
         loop(width // G_TILE, both)
-        if not first:
-            g_exchange(a).start()
 
     def grads_sum(a):
-        g_exchange(a).wait()
         mine, theirs = g_arrays[a][0:2]
 
         def body(m):
+            g_exchange(a, m).wait()
             at = pl.ds(pl.multiple_of(m * G_TILE, G_TILE), G_TILE)
             mine[at, :] = (mine[at, :].astype(F32) + theirs[at, :].astype(F32)).astype(BF16)
 
@@ -487,7 +489,7 @@
                 @pl.when(i >= TURNS)
                 def _():
                     y_copies(i)[0].start()
-        parts = (slice(0, total // 2), slice(total // 2, total))
+        parts = (slice(0, total // 2), slice(0 if text else total // 2, total))
 
         def halves(left, right, part):
             def product(at):
@@ -498,25 +500,26 @@
 
         def middle_and_grads(i):
             middle(i)
+            if text:
+                return
 
             @pl.when(i == 1)
             def _():
-                grads_part(2, halves(dy_s, gb_s, parts[0]), True)
+                grads_part(2, halves(dy_s, gb_s, parts[0]), True, False)
 
             @pl.when(i == 2)
             def _():
-                grads_part(1, halves(a2_s, du_s, parts[0]), True)
+                grads_part(1, halves(a2_s, du_s, parts[0]), True, False)
 
         loop(CHUNKS, middle_and_grads)
-        grads_part(2, halves(dy_s, gb_s, parts[1]), False)
-        grads_part(1, halves(a2_s, du_s, parts[1]), False)
+        grads_part(2, halves(dy_s, gb_s, parts[1]), text, True)
+        grads_part(1, halves(a2_s, du_s, parts[1]), text, True)
         grads_sum(2)
         z_start(2)
         grads_sum(1)
         z_start(1)
         if z_inside:
             z_near(2, upper).start()
-            z_near(1, upper).start()
 
         dq_s, drb_s = gb_s, a2_s
         for s in range(2):
@@ -734,10 +737,6 @@
                 def _():
                     send_c(i - 1)
 
-                @pl.when(i == 3)
-                def _():
-                    grads_part(0, mixed_grads(parts[0]), True)
-
                 @pl.when(i > 2)
                 def _():
                     last(i - 3)
@@ -759,7 +758,7 @@
 
                 @pl.when(i == 2)
                 def _():
-                    grads_part(0, mixed_grads(parts[0]), True)
+                    grads_part(0, mixed_grads(parts[0]), True, False)
 
             loop(CHUNKS, backward)
 
@@ -768,10 +767,11 @@
             for i in range(TURNS, CHUNKS):
                 hand_on(i)
             loop(CHUNKS, lambda i: y_copies(i)[0].start())
-        grads_part(0, mixed_grads(parts[1]), False)
+        grads_part(0, mixed_grads(parts[1]), text, True)
         grads_sum(0)
         z_start(0)
         if z_inside:
+            z_near(1, upper).start()
             z_near(0, upper).start()
         early_start()
         if text:
@@ -781,7 +781,6 @@
             z_middle(0)
             for i in range(TURNS):
                 hand_on(i)
-            loop(CHUNKS, own_y)
         else:
             for i in range(TURNS):
                 y_sum(i)
@@ -792,6 +791,8 @@
             last(CHUNKS - 1)
 
         late_start()
+        if text:
+            loop(CHUNKS, own_y)
         z_finish(2)
         z_finish(1)
         if text:

time: 129 us -> 126 us (0.977)
  Pallas kernels: 125 us -> 122 us
    pallas_call x1, Pallas kernels: 118 us -> 115 us  [per_device(): pl.pallas_call(partial(layers_kernel, rows_i, rows_t, keys_i, dp_size, z_...]
where the time goes in v5:
time: 126 us
  Pallas kernels  122 us (97%)
  local copies, waits for them, and re-layouts  3.56 us (3%)
    pallas_call x1, Pallas kernels, per_device(): pl.pallas_call(partial(layers_kernel, rows_i, rows_t, keys_i, dp_size, z_...  115 us
    pallas_call x1, Pallas kernels, finish_outputs(): pl.pallas_call(partial(finish_kernel, images, keys_i, rows_i), out_shape=...  6.52 us

profile of v5, /device:TPU:0, one launch (start us, length us, event | category | flops | bytes accessed | tf_op | source)
XLA Modules:
  0.0 126.0 jit_solution(2708937858034828344)
XLA Ops:
  0.6 0.0 copy-start
  0.7 1.7 %copy-done = bf16[1,8,197,768]{3,1,2,0:T(8,128)(2,1)S(1)} copy-done((bf16[1,8,197,768]{3,1,2,0:T(8,128)(2,1)S(1)}, bf16[1,8,197,768]{3,1,2,0:T(8,128)(2,1)}, u32[]{:S(2)}) %copy-start) | copy-done | bytes 2420760
  2.3 0.6 constant_dynamic-slice_fusion
  3.0 0.1 copy.26
  3.1 1.1 pad.4
  4.2 115.1 %shard_map.203 = (bf16[1664,768]{1,0:T(8,128)(2,1)}, bf16[1024,768]{1,0:T(8,128)(2,1)}, f32[192,768]{1,0:T(8,128)}, f32[192,768]{1,0:T(8,128)}, f32[192,768]{1,0:T(8,128)}, /*index=5*/f32[16,768]{1,0:T(8,128)}) custom-call(bf16[832,768]{1,0:T(8,128)(2,1)} %bitcast.34, bf16[2,512,768]{2,1,0:T(8,128)(2,1)} %bitcast.37, bf16[576,768]{1,0:T(8,128)(2,1)} %bitcast.40, ...), custom_call_target="tpu_custom_call" | custom-call | tf_op jit(solution)/shard_map/pallas_call | solution.py:972
  119.3 6.5 %shard_map.204 = (bf16[197,8,768]{2,1,0:T(8,128)(2,1)}, bf16[1024,768]{1,0:T(8,128)(2,1)}, f32[2,768]{1,0:T(2,128)}, f32[2,768]{1,0:T(2,128)}, f32[3,192,192]{2,...) custom-call(bf16[8,208,768]{2,1,0:T(8,128)(2,1)} %bitcast.36, ...), custom_call_target="tpu_custom_call" | custom-call | tf_op jit(solution)/shard_map/pallas_call | solution.py:911
Async XLA Ops:
  0.6 1.7 %copy-start = (bf16[1,8,197,768]{3,1,2,0:T(8,128)(2,1)S(1)}, bf16[1,8,197,768]{3,1,2,0:T(8,128)(2,1)}, u32[]{:S(2)}) copy-start(bf16[1,8,197,768]{3,1,2,0:T(8,128)(2,1)} %param.12) | copy-start | bytes 7262212

commit v6 on v5

--- a/solution.py
+++ b/solution.py
@@ -19,6 +19,7 @@
 CHUNKS = 4
 STRIP = 16
 TURNS = 2
+EARLY = 2
 G_TILE = 256
 STEP = 64
 BLOCK = 208
@@ -512,6 +513,8 @@
                 grads_part(1, halves(a2_s, du_s, parts[0]), True, False)
 
         loop(CHUNKS, middle_and_grads)
+        if text:
+            loop(EARLY, lambda i: y_copies(i)[0].start())
         grads_part(2, halves(dy_s, gb_s, parts[1]), text, True)
         grads_part(1, halves(a2_s, du_s, parts[1]), text, True)
         grads_sum(2)
@@ -589,10 +592,16 @@
 
         def dx_copies(i):
             src = rb_s.at[pl.ds(pl.multiple_of(i * rows_t, 16), rows_t)]
-            return remote(src, own_txt(i), K_T1, i, across)
+            return remote(src, yt_s.at[pl.ds(pl.multiple_of(i * rows_t, 16), rows_t)], K_T1, i, across)
 
         def dx_relay(i):
-            return remote(own_txt(i), own_txt(i), K_OT, i, sib)
+            src = yt_s.at[pl.ds(pl.multiple_of(i * rows_t, 16), rows_t)]
+            return local(src, own_txt(i), 12 + i), remote(src, own_txt(i), K_OT, i, sib)
+
+        def dx_hand_on(i):
+            dx_copies(i).wait_recv()
+            for cp in dx_relay(i):
+                cp.start()
 
         if text:
 
@@ -766,7 +775,8 @@
         if text:
             for i in range(TURNS, CHUNKS):
                 hand_on(i)
-            loop(CHUNKS, lambda i: y_copies(i)[0].start())
+            for i in range(EARLY, CHUNKS):
+                y_copies(i)[0].start()
         grads_part(0, mixed_grads(parts[1]), text, True)
         grads_sum(0)
         z_start(0)
@@ -788,6 +798,7 @@
             early_next()
             z_middle(0)
             last(CHUNKS - 2)
+            loop(CHUNKS, dx_hand_on)
             last(CHUNKS - 1)
 
         late_start()
@@ -822,16 +833,14 @@
 
                 else:
                     y_copies(i)[0].wait_send()
-                dx_copies(i).wait_recv()
-                dx_relay(i).start()
+                for cp in dx_relay(i):
+                    cp.wait()
             here, there = img_copies(i)
             here.wait()
             there.wait()
 
         for i in range(CHUNKS):
             finish(i)
-        if not text:
-            loop(CHUNKS, lambda i: dx_relay(i).wait())
         for a in range(3):
             z_end(a)
 

time: 126 us -> 124 us (0.984)
  Pallas kernels: 122 us -> 120 us
    pallas_call x1, Pallas kernels: 115 us -> 113 us  [per_device(): pl.pallas_call(partial(layers_kernel, rows_i, rows_t, keys_i, dp_size, z_...]
where the time goes in v6:
time: 124 us
  Pallas kernels  120 us (97%)
  local copies, waits for them, and re-layouts  3.56 us (3%)
    pallas_call x1, Pallas kernels, per_device(): pl.pallas_call(partial(layers_kernel, rows_i, rows_t, keys_i, dp_size, z_...  113 us
    pallas_call x1, Pallas kernels, finish_outputs(): pl.pallas_call(partial(finish_kernel, images, keys_i, rows_i), out_shape=...  6.52 us

profile of v6, /device:TPU:0, one launch (start us, length us, event | category | flops | bytes accessed | tf_op | source)
XLA Modules:
  0.0 124.0 jit_solution(18436128766573658051)
XLA Ops:
  0.6 0.0 copy-start
  0.7 1.7 %copy-done = bf16[1,8,197,768]{3,1,2,0:T(8,128)(2,1)S(1)} copy-done((bf16[1,8,197,768]{3,1,2,0:T(8,128)(2,1)S(1)}, bf16[1,8,197,768]{3,1,2,0:T(8,128)(2,1)}, u32[]{:S(2)}) %copy-start) | copy-done | bytes 2420760
  2.3 0.6 constant_dynamic-slice_fusion
  3.0 0.1 copy.26
  3.1 1.1 pad.4
  4.2 113.1 %shard_map.203 = (bf16[1664,768]{1,0:T(8,128)(2,1)}, bf16[1024,768]{1,0:T(8,128)(2,1)}, f32[192,768]{1,0:T(8,128)}, f32[192,768]{1,0:T(8,128)}, f32[192,768]{1,0:T(8,128)}, /*index=5*/f32[16,768]{1,0:T(8,128)}) custom-call(bf16[832,768]{1,0:T(8,128)(2,1)} %bitcast.34, bf16[2,512,768]{2,1,0:T(8,128)(2,1)} %bitcast.37, bf16[576,768]{1,0:T(8,128)(2,1)} %bitcast.40, ...), custom_call_target="tpu_custom_call" | custom-call | tf_op jit(solution)/shard_map/pallas_call | solution.py:981
  117.3 6.5 %shard_map.204 = (bf16[197,8,768]{2,1,0:T(8,128)(2,1)}, bf16[1024,768]{1,0:T(8,128)(2,1)}, f32[2,768]{1,0:T(2,128)}, f32[2,768]{1,0:T(2,128)}, f32[3,192,192]{2,...) custom-call(bf16[8,208,768]{2,1,0:T(8,128)(2,1)} %bitcast.36, ...), custom_call_target="tpu_custom_call" | custom-call | tf_op jit(solution)/shard_map/pallas_call | solution.py:920
Async XLA Ops:
  0.6 1.7 %copy-start = (bf16[1,8,197,768]{3,1,2,0:T(8,128)(2,1)S(1)}, bf16[1,8,197,768]{3,1,2,0:T(8,128)(2,1)}, u32[]{:S(2)}) copy-start(bf16[1,8,197,768]{3,1,2,0:T(8,128)(2,1)} %param.12) | copy-start | bytes 7262212

commit v7 on v6

--- a/solution.py
+++ b/solution.py
@@ -166,7 +166,7 @@
             unit, _ = unit_of(x_s[at, :].astype(F32))
             a1_s[at, :] = (unit * gains[0:1, :] + shifts[0:1, :]).astype(BF16)
 
-        loop(CHUNKS, first_norm)
+        first_norm(0)
 
     pl.semaphore_wait(barrier, len(partners))
 
@@ -332,6 +332,8 @@
 
             if text:
                 by_strips(i, first_norm)
+            else:
+                pl.when(i > 0)(lambda: by_strips(i, first_norm))
             left = a1_s[at_rows(i), :]
             lanes = lax.broadcasted_iota(jnp.int32, (1, QKV), 1)
             factor = jnp.where(lanes < WIDE, HEAD**-0.5, 1.0).astype(F32)

time: 124 us -> 124 us (level)
  no operation moved by 1% of the time
where the time goes in v7:
time: 124 us
  Pallas kernels  120 us (97%)
  local copies, waits for them, and re-layouts  3.56 us (3%)
    pallas_call x1, Pallas kernels, per_device(): pl.pallas_call(partial(layers_kernel, rows_i, rows_t, keys_i, dp_size, z_...  113 us
    pallas_call x1, Pallas kernels, finish_outputs(): pl.pallas_call(partial(finish_kernel, images, keys_i, rows_i), out_shape=...  6.52 us

profile of v7, /device:TPU:0, one launch (start us, length us, event | category | flops | bytes accessed | tf_op | source)
XLA Modules:
  0.0 124.1 jit_solution(316518777479925298)
XLA Ops:
  0.6 0.0 copy-start
  0.7 1.7 %copy-done = bf16[1,8,197,768]{3,1,2,0:T(8,128)(2,1)S(1)} copy-done((bf16[1,8,197,768]{3,1,2,0:T(8,128)(2,1)S(1)}, bf16[1,8,197,768]{3,1,2,0:T(8,128)(2,1)}, u32[]{:S(2)}) %copy-start) | copy-done | bytes 2420760
  2.3 0.6 constant_dynamic-slice_fusion
  3.0 0.1 copy.26
  3.1 1.1 pad.4
  4.2 113.2 %shard_map.203 = (bf16[1664,768]{1,0:T(8,128)(2,1)}, bf16[1024,768]{1,0:T(8,128)(2,1)}, f32[192,768]{1,0:T(8,128)}, f32[192,768]{1,0:T(8,128)}, f32[192,768]{1,0:T(8,128)}, /*index=5*/f32[16,768]{1,0:T(8,128)}) custom-call(bf16[832,768]{1,0:T(8,128)(2,1)} %bitcast.34, bf16[2,512,768]{2,1,0:T(8,128)(2,1)} %bitcast.37, bf16[576,768]{1,0:T(8,128)(2,1)} %bitcast.40, ...), custom_call_target="tpu_custom_call" | custom-call | tf_op jit(solution)/shard_map/pallas_call | solution.py:983
  117.4 6.5 %shard_map.204 = (bf16[197,8,768]{2,1,0:T(8,128)(2,1)}, bf16[1024,768]{1,0:T(8,128)(2,1)}, f32[2,768]{1,0:T(2,128)}, f32[2,768]{1,0:T(2,128)}, f32[3,192,192]{2,...) custom-call(bf16[8,208,768]{2,1,0:T(8,128)(2,1)} %bitcast.36, ...), custom_call_target="tpu_custom_call" | custom-call | tf_op jit(solution)/shard_map/pallas_call | solution.py:922
Async XLA Ops:
  0.6 1.7 %copy-start = (bf16[1,8,197,768]{3,1,2,0:T(8,128)(2,1)S(1)}, bf16[1,8,197,768]{3,1,2,0:T(8,128)(2,1)}, u32[]{:S(2)}) copy-start(bf16[1,8,197,768]{3,1,2,0:T(8,128)(2,1)} %param.12) | copy-start | bytes 7262212
